TPU v7x, 128 devices: a whole 4x4x4 slice. The times are simulated.
128 devices in a mesh: dp: 4 (over z_lo, core), fsdp: 32 (over z_hi, x, y).
Axes of the slice: x: 4, y: 4, z: 4 (z_hi: 2, z_lo: 2; z = z_hi * 2 + z_lo), core: 2. Of those that a mesh axis runs over, the one named last changes fastest.
Arguments:
- feat_s: bfloat16 [16384, 6144], P(('dp', 'fsdp')), may hold values from -6 to 6
- feat_t: bfloat16 [16384, 6144], P(('dp', 'fsdp')), may hold values from -6 to 6
- bot_s: float32 [6144, 256], P(('dp', 'fsdp')), may hold values from -0.078125 to 0.078125
- bot_m: float32 [6144, 256], P(('dp', 'fsdp')), may hold values from -0.006 to 0.006
- bot_v: float32 [6144, 256], P(('dp', 'fsdp')), may hold values from 1e-07 to 1e-05
- bot_t: float32 [6144, 256], P(('dp', 'fsdp')), may hold values from -0.078125 to 0.078125
- proto_s: float32 [256, 32768], P(None, ('fsdp', 'dp')), may hold values from -0.1 to 0.1
- proto_m: float32 [256, 32768], P(None, ('fsdp', 'dp')), may hold values from -0.006 to 0.006
- proto_v: float32 [256, 32768], P(None, ('fsdp', 'dp')), may hold values from 1e-07 to 1e-05
- proto_t: float32 [256, 32768], P(None, ('fsdp', 'dp')), may hold values from -0.1 to 0.1
Outputs:
- new_bot_s: float32 [6144, 256], P(('dp', 'fsdp'))
- new_bot_m: float32 [6144, 256], P(('dp', 'fsdp'))
- new_bot_v: float32 [6144, 256], P(('dp', 'fsdp'))
- new_bot_t: float32 [6144, 256], P(('dp', 'fsdp'))
- new_proto_s: float32 [256, 32768], P(None, ('fsdp', 'dp'))
- new_proto_m: float32 [256, 32768], P(None, ('fsdp', 'dp'))
- new_proto_v: float32 [256, 32768], P(None, ('fsdp', 'dp'))
- new_proto_t: float32 [256, 32768], P(None, ('fsdp', 'dp'))
All inputs are finite; a program needn't handle non-finite values.
Results may differ from a plain program's by a relative error of at most 0.0045.
The roundings to bfloat16 on the way count: a program that leaves them out, or rounds other values in their place, can miss the bound.
Values may be sent and summed in bfloat16 or wider, within the bound.
A program may use at most 128 MiB of HBM per device.

v0:
```python
import jax
import jax.numpy as jnp
from jax import lax
from jax.sharding import PartitionSpec as P

tau_student = 0.1
tau_teacher = 0.04
bias_first = 0.99997343860111
bias_second = 0.0952078527


def adamw(param, first, second, grad, teacher):
    first_new = 0.9 * first + 0.1 * grad
    second_new = 0.999 * second + 0.001 * grad * grad
    direction = first_new / bias_first / (jnp.sqrt(second_new / bias_second) + 1e-08)
    param_new = param - 0.002 * (direction + 0.04 * param)
    teacher_new = 0.996 * teacher + 0.004 * param_new
    return (param_new, first_new, second_new, teacher_new)


def per_device(feat_s, feat_t, bot_s, bot_m, bot_v, bot_t, proto_s, proto_m, proto_v, proto_t):
    cols_t = feat_t
    ys = jnp.dot(
        feat_s,
        lax.all_gather(bot_s.astype(jnp.bfloat16), ("dp", "fsdp"), axis=0, tiled=True),
        preferred_element_type=jnp.float32,
    )
    yt = jnp.dot(
        cols_t,
        lax.all_gather(bot_t.astype(jnp.bfloat16), ("dp", "fsdp"), axis=0, tiled=True),
        preferred_element_type=jnp.float32,
    )
    norm_s = jnp.sqrt(jnp.sum(ys * ys, axis=1, keepdims=True) + 1e-06)
    norm_t = jnp.sqrt(jnp.sum(yt * yt, axis=1, keepdims=True) + 1e-06)
    unit_s = ys / norm_s
    codes_s = unit_s.astype(jnp.bfloat16)
    codes_t = (yt / norm_t).astype(jnp.bfloat16)
    half_s = proto_s.astype(jnp.bfloat16)
    half_t = proto_t.astype(jnp.bfloat16)
    cols_s, cols_t = (
        lax.all_gather(half_s, "dp", axis=1, tiled=True),
        lax.all_gather(half_t, "dp", axis=1, tiled=True),
    )
    all_s, all_t = (
        lax.all_gather(codes_s, "fsdp", axis=0, tiled=True),
        lax.all_gather(codes_t, "fsdp", axis=0, tiled=True),
    )
    expo_s = jnp.exp(jnp.dot(all_s, cols_s, preferred_element_type=jnp.float32) / tau_student)
    expo_t = jnp.exp(jnp.dot(all_t, cols_t, preferred_element_type=jnp.float32) / tau_teacher)
    total_s, total_t = lax.psum((jnp.sum(expo_s, axis=1), jnp.sum(expo_t, axis=1)), "fsdp")
    dz = ((expo_s / total_s[:, None] - expo_t / total_t[:, None]) / tau_student).astype(
        jnp.bfloat16
    )
    part_proto = lax.dot_general(
        all_s, dz, (((0,), (0,)), ((), ())), preferred_element_type=jnp.float32
    )
    g_proto = lax.psum_scatter(part_proto, "dp", scatter_dimension=1, tiled=True)
    dh = lax.psum_scatter(
        lax.dot_general(dz, cols_s, (((1,), (1,)), ((), ())), preferred_element_type=jnp.float32),
        "fsdp",
        scatter_dimension=0,
        tiled=True,
    )
    dy = ((dh - unit_s * jnp.sum(unit_s * dh, axis=1, keepdims=True)) / norm_s).astype(jnp.bfloat16)
    g_bot = lax.psum_scatter(
        lax.dot_general(feat_s, dy, (((0,), (0,)), ((), ())), preferred_element_type=jnp.float32),
        ("dp", "fsdp"),
        scatter_dimension=0,
        tiled=True,
    )
    b_s, b_m, b_v, b_t = adamw(bot_s, bot_m, bot_v, g_bot, bot_t)
    p_s, p_m, p_v, p_t = adamw(proto_s, proto_m, proto_v, g_proto, proto_t)
    return (b_s, b_m, b_v, b_t, p_s, p_m, p_v, p_t)


def solution(mesh):
    return jax.shard_map(
        per_device,
        mesh=mesh,
        in_specs=(
            P(("dp", "fsdp"), None),
            P(("dp", "fsdp"), None),
            P(("dp", "fsdp"), None),
            P(("dp", "fsdp"), None),
            P(("dp", "fsdp"), None),
            P(("dp", "fsdp"), None),
            P(None, ("fsdp", "dp")),
            P(None, ("fsdp", "dp")),
            P(None, ("fsdp", "dp")),
            P(None, ("fsdp", "dp")),
        ),
        out_specs=(
            P(("dp", "fsdp"), None),
            P(("dp", "fsdp"), None),
            P(("dp", "fsdp"), None),
            P(("dp", "fsdp"), None),
            P(None, ("fsdp", "dp")),
            P(None, ("fsdp", "dp")),
            P(None, ("fsdp", "dp")),
            P(None, ("fsdp", "dp")),
        ),
        check_vma=False,
    )
```

profile of v0, /device:TPU:0, one launch (start us, length us, event | category | flops | bytes accessed | tf_op | source)
XLA Modules:
  0.0 1882.2 jit_solution(14475440207048507038)
XLA Ops:
  7.2 1.5 convert_element_type.27
  8.9 1.4 convert_element_type.24
  10.4 306.7 %all-gather.9.cloned.1.call-done = bf16[6144,256]{1,0:T(8,128)(2,1)} async-done(((bf16[48,256]{1,0:T(8,128)(2,1)}), bf16[6144,256]{1,0:T(8,128)(2,1)}) %all-gather.9.cloned.1.call-update) | async-done | bytes 3145744 | tf_op jit(solution)/shard_map/all_gather | solution.py:30
  317.1 3.0 multiply_reduce_fusion.1
  320.9 304.2 %all-gather.5.cloned.1.call-done = bf16[6144,256]{1,0:T(8,128)(2,1)} async-done(((bf16[48,256]{1,0:T(8,128)(2,1)}), bf16[6144,256]{1,0:T(8,128)(2,1)}) %all-gather.5.cloned.1.call-update) | async-done | bytes 3145744 | tf_op jit(solution)/shard_map/all_gather | solution.py:25
  625.1 2.5 multiply_reduce_fusion.2
  628.5 7.9 all_gather.20
  636.4 7.3 all_gather.23
  643.7 58.8 %all-gather.11.cloned.1.call-done = bf16[4096,256]{1,0:T(8,128)(2,1)} async-done(((bf16[128,256]{1,0:T(8,128)(2,1)}), bf16[4096,256]{1,0:T(8,128)(2,1)}) %all-gather.11.cloned.1.call-update) | async-done | bytes 2097168 | tf_op jit(solution)/shard_map/all_gather | solution.py:46
  702.6 8.7 fusion.1
  711.2 64.0 %all-gather.7.cloned.1.call-done = bf16[4096,256]{1,0:T(8,128)(2,1)} async-done(((bf16[128,256]{1,0:T(8,128)(2,1)}), bf16[4096,256]{1,0:T(8,128)(2,1)}) %all-gather.7.cloned.1.call-update) | async-done | bytes 2097168 | tf_op jit(solution)/shard_map/all_gather | solution.py:45
  775.2 8.7 fusion
  783.9 178.6 %all-reduce = (f32[4096]{0:T(1024)S(1)}, f32[4096]{0:T(1024)S(1)}) all-reduce(f32[4096]{0:T(1024)S(1)} %get-tuple-element.38, f32[4096]{0:T(1024)S(1)} %get-tuple-element.40), channel_id=1, replica_groups=mesh['dp'=4,'fsdp'=32] {'fsdp'}, use_global_device_ids=true, to_apply=%region_5.0 | all-reduce | flops 8192 | bytes 65536 | tf_op jit(solution)/shard_map/psum | solution.py:50
  962.5 12.5 multiply_convert_fusion
  975.0 3.2 copy-done.1
  978.2 4.6 fusion.9
  983.0 7.5 fusion.10
  990.6 181.4 %reduce-scatter.6.cloned.1.call-done = f32[128,256]{1,0:T(8,128)} async-done(((f32[4096,256]{1,0:T(8,128)}), f32[128,256]{1,0:T(8,128)}) %reduce-scatter.6.cloned.1.call-update) | async-done | bytes 131088 | tf_op jit(solution)/shard_map/reduce_scatter | solution.py:58
  1173.1 4.7 convolution_bitcast_fusion
  1177.7 6.6 copy.39
  1184.4 4.8 reduce-scatter.8.cloned.1.call-done
  1189.2 2.1 multiply_add_fusion
  1191.2 682.6 %reduce-scatter.10.cloned.1.call-done = f32[48,256]{1,0:T(8,128)} async-done(((f32[6144,256]{1,0:T(8,128)}), f32[48,256]{1,0:T(8,128)}) %reduce-scatter.10.cloned.1.call-update) | async-done | bytes 49168 | tf_op jit(solution)/shard_map/reduce_scatter | solution.py:65
  1873.9 1.5 multiply_add_fusion.2
  (40 shorter events, 3.2 us)
Async XLA Ops:
  7.2 617.9 %copy-start = (bf16[128,6144]{1,0:T(8,128)(2,1)S(1)}, bf16[128,6144]{1,0:T(8,128)(2,1)}, u32[]{:S(2)}) copy-start(bf16[128,6144]{1,0:T(8,128)(2,1)} %param.10) | copy-start | bytes 4718596
  7.2 621.3 %copy-start.2 = (f32[256,256]{1,0:T(8,128)S(1)}, f32[256,256]{1,0:T(8,128)}, u32[]{:S(2)}) copy-start(f32[256,256]{1,0:T(8,128)} %param.16) | copy-start | bytes 786436
  7.2 621.3 %copy-start.3 = (f32[256,256]{1,0:T(8,128)S(1)}, f32[256,256]{1,0:T(8,128)}, u32[]{:S(2)}) copy-start(f32[256,256]{1,0:T(8,128)} %param.19) | copy-start | bytes 786436
  7.2 309.9 %all-gather.9.cloned.1.call-start = ((), (), s32[]{:S(2)}) async-start(), calls=%async_computation.5 | async-start | bytes 3170304 | tf_op jit(solution)/shard_map/all_gather | solution.py:30
  8.8 616.3 %all-gather.5.cloned.1.call-start = ((), (), s32[]{:S(2)}) async-start(), calls=%async_computation.3 | async-start | bytes 3170304 | tf_op jit(solution)/shard_map/all_gather | solution.py:25
  10.3 692.2 %all-gather.11.cloned.1.call-start = ((), (), s32[]{:S(2)}) async-start(), calls=%async_computation.6 | async-start | bytes 2162688 | tf_op jit(solution)/shard_map/all_gather | solution.py:46
  320.9 454.3 %all-gather.7.cloned.1.call-start = ((), (), s32[]{:S(2)}) async-start(), calls=%async_computation.4 | async-start | bytes 2162688 | tf_op jit(solution)/shard_map/all_gather | solution.py:45
  628.4 543.6 %reduce-scatter.6.cloned.1.call-start = ((), (), s32[]{:S(2)}) async-start(), calls=%async_computation.7 | async-start | bytes 4325376 | tf_op jit(solution)/shard_map/reduce_scatter | solution.py:58
  975.0 3.2 copy-start.1
  982.8 206.4 %reduce-scatter.8.cloned.1.call-start = ((), (), s32[]{:S(2)}) async-start(), calls=%async_computation.8 | async-start | bytes 1310720 | tf_op jit(solution)/shard_map/reduce_scatter | solution.py:57
  990.5 883.3 %reduce-scatter.10.cloned.1.call-start = ((), (), s32[]{:S(2)}) async-start(), calls=%async_computation.9 | async-start | bytes 6340608 | tf_op jit(solution)/shard_map/reduce_scatter | solution.py:65
  1184.3 4.9 copy-start.4
  1184.3 4.9 copy-start.5
  1184.3 689.5 %copy-start.6 = (f32[48,256]{1,0:T(8,128)S(1)}, f32[48,256]{1,0:T(8,128)}, u32[]{:S(2)}) copy-start(f32[48,256]{1,0:T(8,128)} %param.15) | copy-start | bytes 147460
  1184.3 689.5 %copy-start.7 = (f32[48,256]{1,0:T(8,128)S(1)}, f32[48,256]{1,0:T(8,128)}, u32[]{:S(2)}) copy-start(f32[48,256]{1,0:T(8,128)} %param.12) | copy-start | bytes 147460
  1184.4 689.5 %copy-start.8 = (f32[48,256]{1,0:T(8,128)S(1)}, f32[48,256]{1,0:T(8,128)}, u32[]{:S(2)}) copy-start(f32[48,256]{1,0:T(8,128)} %param.13) | copy-start | bytes 147460
  1184.4 689.5 %copy-start.9 = (f32[48,256]{1,0:T(8,128)S(1)}, f32[48,256]{1,0:T(8,128)}, u32[]{:S(2)}) copy-start(f32[48,256]{1,0:T(8,128)} %param.14) | copy-start | bytes 147460
Sparse Core Ops, SparseCore 0:
  10.3 306.7 all-gather.8
  319.4 305.6 all-gather.4
  628.8 73.7 all-gather.10
  706.1 69.1 all-gather.6
  982.9 189.0 reduce-scatter.5
  1174.2 14.8 reduce-scatter.7
  1191.7 682.1 reduce-scatter.9
where the time goes:
time: 1920 us; the launch traced here: 1880 us
  waiting for transfers between devices  1600 us (83%)
  blocking collectives  194 us (10%)
  matrix products  39.6 us (2%)
  other arithmetic  21.6 us (1%)
    reduce_scatter x1, waiting for transfers between devices, per_device(): lax.psum_scatter(lax.dot_general(feat_s, dy, (((0,), (0,)), ((), ())), pr...  683 us
    all_gather x1, waiting for transfers between devices, per_device(): lax.all_gather(bot_t.astype(jnp.bfloat16), ('dp', 'fsdp'), axis=0, tiled=...  307 us
    all_gather x1, waiting for transfers between devices, per_device(): lax.all_gather(bot_s.astype(jnp.bfloat16), ('dp', 'fsdp'), axis=0, tiled=...  304 us
    reduce_scatter x1, waiting for transfers between devices, per_device(): lax.psum_scatter(lax.dot_general(dz, cols_s, (((1,), (1,)), ((), ())), pr...  181 us
    psum x1, blocking collectives, per_device(): lax.psum((jnp.sum(expo_s, axis=1), jnp.sum(expo_t, axis=1)), 'fsdp')  179 us
    all_gather x1, waiting for transfers between devices, per_device(): lax.all_gather(codes_s, 'fsdp', axis=0, tiled=True)  64 us
    all_gather x1, waiting for transfers between devices, per_device(): lax.all_gather(codes_t, 'fsdp', axis=0, tiled=True)  58.8 us
  transfers between devices with their start and end apart: 7, of which 7 were waited for; matrix products, arithmetic and copies ran while one was open for 2% of the time, Pallas kernels for 0%

commit v1 on v0

v1 whole, which is shorter than its diff:
```python
import math

import jax
import jax.numpy as jnp
from jax import lax
from jax.experimental import pallas as pl
from jax.experimental.pallas import tpu as pltpu
from jax.sharding import PartitionSpec as P

MESH = pl.DeviceIdType.MESH
F32, BF16 = jnp.float32, jnp.bfloat16
tau_student = 0.1
tau_teacher = 0.04
bias_first = 0.99997343860111
bias_second = 0.0952078527
LOG2E = math.log2(math.e)
PB = 256
NB = 8
NP = PB * NB
TB = 128
NT = 16 * TB
PC = 512
SEMS = 112


def adamw(param, first, second, grad, teacher):
    first_new = 0.9 * first + 0.1 * grad
    second_new = 0.999 * second + 0.001 * grad * grad
    direction = first_new / bias_first / (jnp.sqrt(second_new / bias_second) + 1e-08)
    param_new = param - 0.002 * (direction + 0.04 * param)
    teacher_new = 0.996 * teacher + 0.004 * param_new
    return (param_new, first_new, second_new, teacher_new)


def run(*steps):
    steps = list(steps)
    while steps:
        for step in list(steps):
            try:
                next(step)
            except StopIteration:
                steps.remove(step)


def dot(a, b, dims=((1,), (0,))):
    return lax.dot_general(a, b, (dims, ((), ())), preferred_element_type=F32)


def kernel(
    feat_s, feat_t, bot_s, bot_t, proto_s, proto_t,
    g_bot, g_proto,
    w, fx, yf, yr, unit, norm, cs, ct, ps, pt, pn, es, et, dz,
    tx, ty, tot, dh0, dhr0, dh1, dhr1, grecv, gz, gzr,
    dy, b0, br0, b1, br1, b2, br2,
    send_sem, recv_sem, local_sem,
):
    dp, fs = lax.axis_index("dp"), lax.axis_index("fsdp")
    core, zl = lax.rem(dp, 2), lax.div(dp, 2)
    zh, x, y = lax.div(fs, 16), lax.rem(lax.div(fs, 4), 4), lax.rem(fs, 4)
    z = zh * 2 + zl
    other = 1 - core
    turn = 1 + 2 * core

    def device(x=x, y=y, z=z, core=core):
        return {"dp": lax.rem(z, 2) * 2 + core, "fsdp": lax.div(z, 2) * 16 + x * 4 + y}

    place = {"x": x, "y": y, "z": z}

    def ring(axis):
        at = place[axis]
        ahead, behind = lax.rem(at + turn, 4), lax.rem(at + 4 - turn, 4)
        return at, ahead, behind, lax.rem(at + 2, 4)

    copies = []

    def push(src, dst, to):
        at = len(copies)
        copy = pltpu.make_async_remote_copy(
            src_ref=src, dst_ref=dst, send_sem=send_sem.at[at], recv_sem=recv_sem.at[at],
            device_id=to, device_id_type=MESH,
        )
        copy.start()
        copies.append(copy)
        return copy

    def gather(axis, block):
        at, ahead, behind, _ = ring(axis)
        up = push(block(at), block(at), device(**{axis: ahead}))
        down = push(block(at), block(at), device(**{axis: behind}))
        yield
        up.wait_recv()
        on = push(block(behind), block(behind), device(**{axis: ahead}))
        yield
        down.wait_recv()
        on.wait_recv()

    def scatter(axis, parts, recv, put):
        at, ahead, behind, far = ring(axis)
        up = push(parts.at[far], recv.at[0], device(**{axis: ahead}))
        down = push(parts.at[behind], recv.at[1], device(**{axis: behind}))
        yield
        up.wait_recv()
        parts[ahead] = (parts[ahead].astype(F32) + recv[0].astype(F32)).astype(parts.dtype)
        on = push(parts.at[ahead], recv.at[2], device(**{axis: ahead}))
        yield
        down.wait_recv()
        total = parts[at].astype(F32) + recv[1].astype(F32)
        on.wait_recv()
        put(total + recv[2].astype(F32))

    barrier = pltpu.get_barrier_semaphore()
    peers = [device(core=other)]
    for axis in ("x", "y", "z"):
        for step in (1, 3) if axis == "z" else (1, 2, 3):
            peers.append(device(**{axis: lax.rem(place[axis] + step, 4)}))
    for peer in peers:
        pl.semaphore_signal(barrier, inc=1, device_id=peer, device_id_type=MESH)

    local = []
    for side, feat in enumerate((feat_s, feat_t)):
        for half in range(2):
            columns = pl.ds(pl.multiple_of((half * 2 + core) * 1536, 1536), 1536)
            rows = pl.ds(pl.multiple_of(core * TB, TB), TB)
            copy = pltpu.make_async_copy(
                feat.at[:, columns], fx.at[side, half, rows, :], local_sem.at[side * 2 + half]
            )
            copy.start()
            local.append(copy)
    w[zl, zh, x, y, :, 0:256] = bot_s[...].astype(BF16)
    w[zl, zh, x, y, :, 256:512] = bot_t[...].astype(BF16)
    pl.semaphore_wait(barrier, len(peers))

    def part(k):
        return pl.ds(16 * k, 16)

    def bot_gather(k):
        r = part(k)
        if k == 0:
            yield from gather("x", lambda c: w.at[zl, zh, c, y, r, :])
            yield from gather("y", lambda c: w.at[zl, zh, :, c, r, :])
            yield from gather("z", lambda c: w.at[lax.rem(c, 2), lax.div(c, 2), :, :, r, :])
        elif k == 1:
            yield from gather("y", lambda c: w.at[zl, zh, x, c, r, :])
            yield from gather("z", lambda c: w.at[lax.rem(c, 2), lax.div(c, 2), x, :, r, :])
            yield from gather("x", lambda c: w.at[:, :, c, :, r, :])
        else:
            yield from gather("z", lambda c: w.at[lax.rem(c, 2), lax.div(c, 2), x, y, r, :])
            yield from gather("x", lambda c: w.at[:, :, c, y, r, :])
            yield from gather("y", lambda c: w.at[:, :, :, c, r, :])

    def features():
        got = []
        for side, feat in enumerate((feat_s, feat_t)):
            for half in range(2):
                columns = pl.ds(pl.multiple_of((half * 2 + other) * 1536, 1536), 1536)
                rows = pl.ds(pl.multiple_of(core * TB, TB), TB)
                got.append(push(feat.at[:, columns], fx.at[side, half, rows, :], device(core=other)))
        ps[z, core] = proto_s[...].T.astype(BF16)
        pt[z, core] = proto_t[...].T.astype(BF16)
        yield
        yield
        for copy in got:
            copy.wait_recv()
        for copy in local:
            copy.wait()

    run(bot_gather(0), bot_gather(1), bot_gather(2), features())
    gathered = list(copies)

    proto_steps = [gather("z", lambda c: ps.at[c, core]), gather("z", lambda c: pt.at[c, core])]
    for step in proto_steps:
        next(step)

    for side in range(2):
        total = jnp.zeros((2 * TB, 256), F32)
        for a in range(2):
            for b in range(2):
                block = w[a, b, :, :, :, pl.ds(256 * side, 256)].reshape(768, 256)
                total += dot(fx[side, a, :, pl.ds(768 * b, 768)], block)
        yf[side, 0] = total[:TB]
        yf[side, 1] = total[TB:]
    swap = push(yf.at[:, other], yr, device(core=other))
    for step in proto_steps:
        next(step)
    swap.wait_recv()
    for side in range(2):
        yt = (yf[side, core] + yr[side]).T
        n = jnp.sqrt(jnp.sum(yt * yt, axis=0, keepdims=True) + 1e-06)
        u = yt / n
        if side == 0:
            unit[...] = u
            norm[0:1, :] = n
        (cs, ct)[side][x, y] = u.T.astype(BF16)

    def codes(side):
        if side == 0:
            yield from gather("x", lambda c: cs.at[c, y])
            yield from gather("y", lambda c: cs.at[:, c])
        else:
            yield from gather("y", lambda c: ct.at[x, c])
            yield from gather("x", lambda c: ct.at[c])

    def transposed():
        for copy in gathered:
            copy.wait_send()
        for a in range(2):
            for b in range(2):
                block = fx[0, a, :, pl.ds(768 * b, 768)].T
                w[a, b, :, :, :, 0:256] = block.reshape(4, 4, 48, 256)
        yield

    def protos():
        yield
        for step in proto_steps:
            run(step)
        swaps = [push(ref.at[:, core], ref.at[:, core], device(core=other)) for ref in (ps, pt)]
        yield
        yield
        for copy in swaps:
            copy.wait_recv()
        for b in range(NB):
            pn[:, b * PB : (b + 1) * PB] = ps[b // 2, b % 2].T

    run(codes(0), codes(1), transposed(), protos())

    blocks = PC // PB
    for side, (code, proto, out, scale) in enumerate(
        ((cs, ps, es, LOG2E / tau_student), (ct, pt, et, LOG2E / tau_teacher))
    ):

        def tokens(i, _, side=side, code=code, proto=proto, out=out, scale=scale):
            a, b = lax.div(i, 2), lax.rem(i, 2) * 2
            c = code[a, pl.ds(b, 2)].reshape(2 * TB, 256)

            def some(j, total):
                p = proto[j].reshape(PC, 256)
                e = jnp.exp2(dot(p, c, ((1,), (1,))) * scale)
                out[i, pl.ds(pl.multiple_of(j * PC, PC), PC), :] = e
                return total + jnp.sum(e.reshape(PC // 8, 8, 2 * TB), axis=0)

            total = lax.fori_loop(0, NP // PC, some, jnp.zeros((8, 2 * TB), F32))
            total = jnp.sum(total, axis=0, keepdims=True)
            tx[x, side, pl.ds(i * 2, 1), :] = total[:, :TB]
            tx[x, side, pl.ds(i * 2 + 1, 1), :] = total[:, TB:]
            return 0

        lax.fori_loop(0, NT // (2 * TB), tokens, 0)

    sent = [push(tx.at[x], tx.at[x], device(x=lax.rem(x + d, 4))) for d in (1, 2, 3)]
    for copy in sent:
        copy.wait_recv()
    ty[y] = tx[0] + tx[1] + tx[2] + tx[3]
    sent = [push(ty.at[y], ty.at[y], device(y=lax.rem(y + d, 4))) for d in (1, 2, 3)]
    for copy in sent:
        copy.wait_recv()
    tot[...] = (1.0 / tau_student) / (ty[0] + ty[1] + ty[2] + ty[3])

    def back(i, _):
        inv_s = jnp.concatenate([tot[0, pl.ds(2 * i, 1), :], tot[0, pl.ds(2 * i + 1, 1), :]], 1)
        inv_t = jnp.concatenate([tot[1, pl.ds(2 * i, 1), :], tot[1, pl.ds(2 * i + 1, 1), :]], 1)
        columns = pl.ds(pl.multiple_of(i * 2 * TB, 2 * TB), 2 * TB)

        def some(j, _):
            rows = pl.ds(pl.multiple_of(j * PC, PC), PC)
            dz[rows, columns] = (es[i, rows, :] * inv_s - et[i, rows, :] * inv_t).astype(BF16)
            return 0

        lax.fori_loop(0, NP // PC, some, 0)
        dh = dot(pn[...], dz[:, columns])
        a, b = lax.div(i, 2), lax.rem(i, 2) * 2
        for d in range(2):
            dh0[0, a, b + d] = dh[:128, d * TB : (d + 1) * TB].astype(BF16)
            dh0[1, b + d, a] = dh[128:, d * TB : (d + 1) * TB].astype(BF16)
        return 0

    lax.fori_loop(0, NT // (2 * TB), back, 0)

    def dh_scatter(k):
        def middle(v):
            dh1[k] = v

        def last(v):
            dhr1[k, 0] = v

        yield from scatter("xy"[k], dh0.at[k], dhr0.at[k], middle)
        yield from scatter("yx"[k], dh1.at[k], dhr1.at[k], last)

    def proto_grad():
        def grad(block):
            rows = pl.ds(pl.multiple_of(block * PB, PB), PB)
            return dot(dz[rows, :], cs[...].reshape(NT, 256))

        def theirs(i, _):
            es[0, pl.ds(pl.multiple_of(i * PB, PB), PB), :] = grad(i * 2 + other)
            return 0

        def ours(i, _):
            es[1, pl.ds(pl.multiple_of(i * PB, PB), PB), :] = grad(i * 2 + core)
            return 0

        lax.fori_loop(0, 4, theirs, 0)
        swap = push(es.at[0, pl.ds(0, 4 * PB), :], grecv, device(core=other))
        yield
        lax.fori_loop(0, 4, ours, 0)
        swap.wait_recv()
        gz[...] = (es[1, : 4 * PB, :] + grecv[...]).astype(BF16).reshape(4, PB, 256)

        def last(v):
            g_proto[...] = v.T

        yield from scatter("z", gz, gzr, last)

    proto_steps = proto_grad()
    run(dh_scatter(0), dh_scatter(1), proto_steps)

    dht = jnp.concatenate([dhr1[0, 0], dhr1[1, 0]], axis=0)
    u = unit[...]
    dyt = (dht - u * jnp.sum(u * dht, axis=0, keepdims=True)) / norm[0:1, :]
    dy[core] = dyt.astype(BF16)
    swap = push(dy.at[core], dy.at[core], device(core=other))
    swap.wait_recv()

    dyb = jnp.concatenate([dy[0], dy[1]], axis=1)
    for a in range(2):
        for b in range(2):
            c = b * 2 + a
            g = dot(w[a, b, :, :, :, 0:256].reshape(768, 256), dyb, ((1,), (1,))).astype(BF16)
            g = g.reshape(4, 4, 48, 256)
            for i in range(4):
                for j in range(4):
                    b0[0, i, j, c] = g[i, j, 0:16]
                    b0[1, j, c, i] = g[i, j, 16:32]
                    b0[2, c, i, j] = g[i, j, 32:48]

    def bot_scatter(k):
        def first(v):
            b1[k] = v

        def second(v):
            b2[k] = v

        def last(v):
            g_bot[16 * k : 16 * (k + 1), :] = v

        one, two, three = ("xyz", "yzx", "zxy")[k]
        yield from scatter(one, b0.at[k], br0.at[k], first)
        yield from scatter(two, b1.at[k], br1.at[k], second)
        yield from scatter(three, b2.at[k], br2.at[k], last)

    run(bot_scatter(0), bot_scatter(1), bot_scatter(2))
    for copy in copies[len(gathered) :]:
        copy.wait_send()


def gradients(feat_s, feat_t, bot_s, bot_t, proto_s, proto_t):
    whole = pl.BlockSpec(memory_space=pltpu.VMEM)
    vmem = pltpu.VMEM
    return pl.pallas_call(
        kernel,
        out_shape=(
            jax.ShapeDtypeStruct((48, 256), F32),
            jax.ShapeDtypeStruct((256, PB), F32),
        ),
        in_specs=[pl.BlockSpec(memory_space=pl.ANY)] * 2 + [whole] * 4,
        out_specs=(whole, whole),
        scratch_shapes=[
            vmem((2, 2, 4, 4, 48, 512), BF16),
            vmem((2, 2, 2 * TB, 1536), BF16),
            vmem((2, 2, TB, 256), F32),
            vmem((2, TB, 256), F32),
            vmem((256, TB), F32),
            vmem((8, TB), F32),
            vmem((4, 4, TB, 256), BF16),
            vmem((4, 4, TB, 256), BF16),
            vmem((4, 2, PB, 256), BF16),
            vmem((4, 2, PB, 256), BF16),
            vmem((256, NP), BF16),
            vmem((8, NP, 2 * TB), F32),
            vmem((8, NP, 2 * TB), F32),
            vmem((NP, NT), BF16),
            vmem((4, 2, 16, TB), F32),
            vmem((4, 2, 16, TB), F32),
            vmem((2, 16, TB), F32),
            vmem((2, 4, 4, 128, TB), BF16),
            vmem((2, 3, 4, 128, TB), BF16),
            vmem((2, 4, 128, TB), F32),
            vmem((2, 3, 128, TB), F32),
            vmem((4 * PB, 256), F32),
            vmem((4, PB, 256), BF16),
            vmem((3, PB, 256), BF16),
            vmem((2, 256, TB), BF16),
            vmem((3, 4, 4, 4, 16, 256), BF16),
            vmem((3, 3, 4, 4, 16, 256), BF16),
            vmem((3, 4, 4, 16, 256), F32),
            vmem((3, 3, 4, 16, 256), F32),
            vmem((3, 4, 16, 256), F32),
            vmem((3, 3, 16, 256), F32),
            pltpu.SemaphoreType.DMA((SEMS,)),
            pltpu.SemaphoreType.DMA((SEMS,)),
            pltpu.SemaphoreType.DMA((4,)),
        ],
        compiler_params=pltpu.CompilerParams(
            collective_id=0, has_side_effects=True, vmem_limit_bytes=63 * 1024 * 1024
        ),
    )(feat_s, feat_t, bot_s, bot_t, proto_s, proto_t)


def per_device(feat_s, feat_t, bot_s, bot_m, bot_v, bot_t, proto_s, proto_m, proto_v, proto_t):
    g_bot, g_proto = gradients(feat_s, feat_t, bot_s, bot_t, proto_s, proto_t)
    return adamw(bot_s, bot_m, bot_v, g_bot, bot_t) + adamw(
        proto_s, proto_m, proto_v, g_proto, proto_t
    )


def solution(mesh):
    rows, columns = P(("dp", "fsdp"), None), P(None, ("fsdp", "dp"))
    return jax.shard_map(
        per_device,
        mesh=mesh,
        in_specs=(rows,) * 6 + (columns,) * 4,
        out_specs=(rows,) * 4 + (columns,) * 4,
        check_vma=False,
    )
```

time: 1920 us -> 138 us (0.07); the launches traced: 1880 us -> 138 us
  waiting for transfers between devices: 1600 us -> 0 us
  blocking collectives: 194 us -> 0 us
  Pallas kernels: 0 us -> 134 us
  matrix products: 39.6 us -> 0 us
    reduce_scatter x3 -> x0, waiting for transfers between devices: 869 us -> none  [the longest x1 683 us: per_device(): lax.psum_scatter(lax.dot_general(feat_s, dy, (((0,), (0,)), ((), ())), pr...]
    all_gather x4 -> x0, waiting for transfers between devices: 734 us -> none  [the longest x1 307 us: per_device(): lax.all_gather(bot_t.astype(jnp.bfloat16), ('dp', 'fsdp'), axis=0, tiled=...]
    psum x1 -> x0, blocking collectives: 179 us -> none  [per_device(): lax.psum((jnp.sum(expo_s, axis=1), jnp.sum(expo_t, axis=1)), 'fsdp')]
    pallas_call x0 -> x1, Pallas kernels: none -> 134 us  [gradients(): pl.pallas_call(kernel, out_shape=(jax.ShapeDtypeStruct((48, 256), F32), j...]
    dot_general x7 -> x0, matrix products: 39.6 us -> none  [the longest x1 8.68 us: per_device(): jnp.dot(all_t, cols_t, preferred_element_type=jnp.float32) / tau_teacher]
  transfers between devices with their start and end apart: 7 -> 0, of which waited for: 7 -> 0; matrix products, arithmetic and copies ran while one was open for 2% -> 0% of each run, Pallas kernels for 0% -> 0%
where the time goes in v1:
time: 138 us
  Pallas kernels  134 us (97%)
  other arithmetic  2.86 us (2%)
    pallas_call x1, Pallas kernels, gradients(): pl.pallas_call(kernel, out_shape=(jax.ShapeDtypeStruct((48, 256), F32), j...  134 us
    add x2, other arithmetic, adamw(): teacher_new = 0.996 * teacher + 0.004 * param_new  2.86 us

profile of v1, /device:TPU:0, one launch (start us, length us, event | category | flops | bytes accessed | tf_op | source)
XLA Modules:
  0.0 137.7 jit_solution(2528347784603208692)
XLA Ops:
  0.6 0.0 copy-start
  0.6 0.0 copy-start.1
  0.7 0.0 copy-start.2
  0.7 134.1 %shard_map.161 = (f32[48,256]{1,0:T(8,128)}, f32[256,256]{1,0:T(8,128)}) custom-call(bf16[128,6144]{1,0:T(8,128)(2,1)} %feat_s.1, bf16[128,6144]{1,0:T(8,128)(2,1)} %feat_t.1, f32[48,256]{1,0:T(8,128)} %bot_s.1, f32[48,256]{1,0:T(8,128)} %bot_t.1, f32[256,256]{1,0:T(8,128)} %proto_s.1, f32[256,256]{1,0:T(8,128)} %proto_t.1), custom_call_target="tpu_custom_call" | custom-call | tf_op jit(solution)/shard_map/pallas_call | solution.py:358
  134.8 0.0 copy-start.3
  134.8 0.0 copy-start.4
  134.8 0.0 copy-start.5
  134.8 0.0 copy-start.6
  134.8 0.0 copy-start.7
  134.8 0.0 copy-done
  134.8 0.0 copy-done.1
  134.8 0.0 copy-done.2
  134.9 2.2 %multiply_add_fusion = (f32[256,256]{1,0:T(8,128)}, f32[256,256]{1,0:T(8,128)}, f32[256,256]{1,0:T(8,128)}, f32[256,256]{1,0:T(8,128)}) fusion(f32[256,256]{1,0:T(8,128)S(1)} %copy-done.1, f32[256,256]{1,0:T(8,128)S(1)} %copy-done, f32[256,256]{1,0:T(8,128)} %get-tuple-element.11, f32[256,256]{1,0:T(8,128)S(1)} %copy-done.2, f32[256,256]{1,0:T(8,128)} %param.18), kind=kLoop, calls=%fused_computation.2 | loop fusion | flops 1179648 | bytes 2359296 | tf_op jit(solution)/shard_map/add | solution.py:31
  137.0 0.0 copy-done.3
  137.0 0.0 copy-done.4
  137.0 0.0 copy-done.5
  137.0 0.0 copy-done.6
  137.0 0.0 copy-done.7
  137.0 0.7 multiply_add_fusion.2
Async XLA Ops:
  0.6 134.2 %copy-start = (f32[256,256]{1,0:T(8,128)S(1)}, f32[256,256]{1,0:T(8,128)}, u32[]{:S(2)}) copy-start(f32[256,256]{1,0:T(8,128)} %proto_s.1) | copy-start | bytes 786436
  0.6 134.2 %copy-start.1 = (f32[256,256]{1,0:T(8,128)S(1)}, f32[256,256]{1,0:T(8,128)}, u32[]{:S(2)}) copy-start(f32[256,256]{1,0:T(8,128)} %proto_t.1) | copy-start | bytes 786436
  0.7 134.2 %copy-start.2 = (f32[256,256]{1,0:T(8,128)S(1)}, f32[256,256]{1,0:T(8,128)}, u32[]{:S(2)}) copy-start(f32[256,256]{1,0:T(8,128)} %param.17) | copy-start | bytes 786436
  134.8 2.3 %copy-start.3 = (f32[48,256]{1,0:T(8,128)S(1)}, f32[48,256]{1,0:T(8,128)}, u32[]{:S(2)}) copy-start(f32[48,256]{1,0:T(8,128)} %bot_t.1) | copy-start | bytes 147460
  134.8 2.2 %copy-start.4 = (f32[48,256]{1,0:T(8,128)S(1)}, f32[48,256]{1,0:T(8,128)}, u32[]{:S(2)}) copy-start(f32[48,256]{1,0:T(8,128)} %bot_s.1) | copy-start | bytes 147460
  134.8 2.2 %copy-start.5 = (f32[48,256]{1,0:T(8,128)S(1)}, f32[48,256]{1,0:T(8,128)}, u32[]{:S(2)}) copy-start(f32[48,256]{1,0:T(8,128)} %param.13) | copy-start | bytes 147460
  134.8 2.2 %copy-start.6 = (f32[48,256]{1,0:T(8,128)S(1)}, f32[48,256]{1,0:T(8,128)}, u32[]{:S(2)}) copy-start(f32[48,256]{1,0:T(8,128)} %param.14) | copy-start | bytes 147460
  134.8 2.2 %copy-start.7 = (f32[48,256]{1,0:T(8,128)S(1)}, f32[48,256]{1,0:T(8,128)}, u32[]{:S(2)}) copy-start(f32[48,256]{1,0:T(8,128)} %get-tuple-element.10) | copy-start | bytes 147460

commit v2 on v1

v2 whole, which is shorter than its diff:
```python
import math

import jax
import jax.numpy as jnp
from jax import lax
from jax.experimental import pallas as pl
from jax.experimental.pallas import tpu as pltpu
from jax.sharding import PartitionSpec as P

MESH = pl.DeviceIdType.MESH
F32, BF16 = jnp.float32, jnp.bfloat16
tau_student = 0.1
tau_teacher = 0.04
bias_first = 0.99997343860111
bias_second = 0.0952078527
LOG2E = math.log2(math.e)
PB = 256
NB = 8
NP = PB * NB
TB = 128
NT = 16 * TB
SEMS = 160


def adamw(param, first, second, grad, teacher):
    first_new = 0.9 * first + 0.1 * grad
    second_new = 0.999 * second + 0.001 * grad * grad
    direction = first_new / bias_first / (jnp.sqrt(second_new / bias_second) + 1e-08)
    param_new = param - 0.002 * (direction + 0.04 * param)
    teacher_new = 0.996 * teacher + 0.004 * param_new
    return (param_new, first_new, second_new, teacher_new)


def together(*steps):
    steps = list(steps)
    while steps:
        for step in list(steps):
            try:
                next(step)
            except StopIteration:
                steps.remove(step)
        yield


def run(*steps):
    for _ in together(*steps):
        pass


def dot(a, b, dims=((1,), (0,))):
    return lax.dot_general(a, b, (dims, ((), ())), preferred_element_type=F32)


def kernel(
    feat_s, feat_t, bot_s, bot_t, proto_s, proto_t,
    g_bot, g_proto,
    w, fx, yf, yr, unit, norm, cs, ct, ps, pt, pn, es, et, dz,
    tx, ty, tot, dh0, dhr0, dh1, dhr1, dht, grecv, gz, gzr,
    dy, b0, br0, b1, br1, b2, br2,
    send_sem, recv_sem, local_sem,
):
    dp, fs = lax.axis_index("dp"), lax.axis_index("fsdp")
    core, zl = lax.rem(dp, 2), lax.div(dp, 2)
    zh, x, y = lax.div(fs, 16), lax.rem(lax.div(fs, 4), 4), lax.rem(fs, 4)
    z = zh * 2 + zl
    other = 1 - core
    turn = 1 + 2 * core

    def device(x=x, y=y, z=z, core=core):
        return {"dp": lax.rem(z, 2) * 2 + core, "fsdp": lax.div(z, 2) * 16 + x * 4 + y}

    place = {"x": x, "y": y, "z": z}

    def ring(axis):
        at = place[axis]
        ahead, behind = lax.rem(at + turn, 4), lax.rem(at + 4 - turn, 4)
        return at, ahead, behind, lax.rem(at + 2, 4)

    copies = []

    def push(src, dst, to, log=None):
        at = len(copies)
        copy = pltpu.make_async_remote_copy(
            src_ref=src, dst_ref=dst, send_sem=send_sem.at[at], recv_sem=recv_sem.at[at],
            device_id=to, device_id_type=MESH,
        )
        copy.start()
        copies.append(copy)
        if log is not None:
            log.append(copy)
        return copy

    def gather(axis, block, log=None):
        at, ahead, behind, _ = ring(axis)
        up = push(block(at), block(at), device(**{axis: ahead}), log)
        down = push(block(at), block(at), device(**{axis: behind}), log)
        yield
        up.wait_recv()
        on = push(block(behind), block(behind), device(**{axis: ahead}), log)
        yield
        down.wait_recv()
        on.wait_recv()

    def spread(axis, block, log=None):
        at = place[axis]
        sent = []
        for d in (2, 1, 3):
            sent.append(push(block(at), block(at), device(**{axis: lax.rem(at + d, 4)}), log))
        yield
        for copy in sent:
            copy.wait_recv()

    def scatter(axis, parts, recv, put):
        at = place[axis]
        sent = []
        for i, d in enumerate((2, 1, 3)):
            to = lax.rem(at + d, 4)
            sent.append(push(parts.at[to], recv.at[i], device(**{axis: to})))
        yield
        total = parts[at].astype(F32)
        for i, copy in enumerate(sent):
            copy.wait_recv()
            total += recv[i].astype(F32)
        put(total)

    barrier = pltpu.get_barrier_semaphore()
    peers = [device(core=other)]
    for axis in ("x", "y", "z"):
        for step in (1, 2, 3):
            peers.append(device(**{axis: lax.rem(place[axis] + step, 4)}))
    for peer in peers:
        pl.semaphore_signal(barrier, inc=1, device_id=peer, device_id_type=MESH)

    local = []
    for side, feat in enumerate((feat_s, feat_t)):
        for half in range(2):
            columns = pl.ds(pl.multiple_of((half * 2 + core) * 1536, 1536), 1536)
            rows = pl.ds(pl.multiple_of(core * TB, TB), TB)
            copy = pltpu.make_async_copy(
                feat.at[:, columns], fx.at[side, half, rows, :], local_sem.at[side * 2 + half]
            )
            copy.start()
            local.append(copy)
    w[zl, zh, x, y, :, 0:256] = bot_s[...].astype(BF16)
    w[zl, zh, x, y, :, 256:512] = bot_t[...].astype(BF16)
    pl.semaphore_wait(barrier, len(peers))

    def part(k):
        return pl.ds(16 * k, 16)

    mine = {0: [], 1: []}

    def bot_gather(k, side):
        r, c = part(k), pl.ds(256 * side, 256)

        def at_z(i):
            return lax.rem(i, 2), lax.div(i, 2)

        log = mine[side]
        if k == 0:
            yield from spread("x", lambda i: w.at[zl, zh, i, y, r, c], log)
            yield from spread("y", lambda i: w.at[zl, zh, :, i, r, c], log)
            yield from gather("z", lambda i: w.at[(*at_z(i), slice(None), slice(None), r, c)], log)
        elif k == 1:
            yield from spread("y", lambda i: w.at[zl, zh, x, i, r, c], log)
            yield from spread("z", lambda i: w.at[(*at_z(i), x, slice(None), r, c)], log)
            yield from gather("x", lambda i: w.at[:, :, i, :, r, c], log)
        else:
            yield from spread("z", lambda i: w.at[(*at_z(i), x, y, r, c)], log)
            yield from spread("x", lambda i: w.at[:, :, i, y, r, c], log)
            yield from gather("y", lambda i: w.at[:, :, :, i, r, c], log)

    features = []
    for side, feat in enumerate((feat_s, feat_t)):
        for half in range(2):
            columns = pl.ds(pl.multiple_of((half * 2 + other) * 1536, 1536), 1536)
            rows = pl.ds(pl.multiple_of(core * TB, TB), TB)
            features.append((side, feat.at[:, columns], fx.at[side, half, rows, :]))
    got = {}

    def projected(side):
        yield from together(*(bot_gather(k, side) for k in range(3)))
        for copy in got[side]:
            copy.wait_recv()
        for copy in local[2 * side : 2 * side + 2]:
            copy.wait()
        total = jnp.zeros((2 * TB, 256), F32)
        for a in range(2):
            for b in range(2):
                block = w[a, b, :, :, :, pl.ds(256 * side, 256)].reshape(768, 256)
                total += dot(fx[side, a, :, pl.ds(768 * b, 768)], block)
        yf[side, 0] = total[:TB]
        yf[side, 1] = total[TB:]
        swap = push(yf.at[side, other], yr.at[side], device(core=other))
        yield
        swap.wait_recv()
        yt = (yf[side, core] + yr[side]).T
        n = jnp.sqrt(jnp.sum(yt * yt, axis=0, keepdims=True) + 1e-06)
        u = yt / n
        if side == 0:
            unit[...] = u
            norm[0:1, :] = n
        (cs, ct)[side][x, y] = u.T.astype(BF16)

    def exponentials(side, line):
        code, proto, out, scale = (
            (cs, ps, es, LOG2E / tau_student),
            (ct, pt, et, LOG2E / tau_teacher),
        )[side]

        def pair(q, _):
            if side == 0:
                c = code[pl.ds(2 * q, 2), line].reshape(2 * TB, 256)
            else:
                c = code[line, pl.ds(2 * q, 2)].reshape(2 * TB, 256)
            total = jnp.zeros((8, 2 * TB), F32)
            for b in range(NB):
                rows = pl.ds(b * PB, PB)
                e = jnp.exp2(dot(proto[b // 2, b % 2], c, ((1,), (1,))) * scale)
                if side == 0:
                    columns = pl.ds(pl.multiple_of(lax.rem(line, 2) * TB, TB), TB)
                    out[2 * q, lax.div(line, 2), rows, columns] = e[:, :TB]
                    out[2 * q + 1, lax.div(line, 2), rows, columns] = e[:, TB:]
                else:
                    out[line, q, rows, :] = e
                total += jnp.sum(e.reshape(PB // 8, 8, 2 * TB), axis=0)
            total = jnp.sum(total, axis=0, keepdims=True)
            if side == 0:
                tx[x, side, pl.ds(8 * q + line, 1), :] = total[:, :TB]
                tx[x, side, pl.ds(8 * q + 4 + line, 1), :] = total[:, TB:]
            else:
                tx[x, side, pl.ds(4 * line + 2 * q, 1), :] = total[:, :TB]
                tx[x, side, pl.ds(4 * line + 2 * q + 1, 1), :] = total[:, TB:]
            return 0

        lax.fori_loop(0, 2, pair, 0)

    def forward(side):
        yield from projected(side)
        if side == 0:
            yield from spread("x", lambda i: cs.at[i, y])
            axis, block = "y", lambda i, h: cs.at[pl.ds(2 * h, 2), i]
        else:
            yield from spread("y", lambda i: ct.at[x, i])
            axis, block = "x", lambda i, h: ct.at[i, pl.ds(2 * h, 2)]
        at, ahead, behind, far = ring(axis)
        up = [push(block(at, h), block(at, h), device(**{axis: ahead})) for h in range(2)]
        down = [push(block(at, h), block(at, h), device(**{axis: behind})) for h in range(2)]
        yield
        on = []
        for h in range(2):
            up[h].wait_recv()
            on.append(push(block(behind, h), block(behind, h), device(**{axis: ahead})))
        yield
        exponentials(side, at)
        exponentials(side, behind)
        yield
        for copy in down:
            copy.wait_recv()
        exponentials(side, ahead)
        yield
        for copy in on:
            copy.wait_recv()
        exponentials(side, far)

    def beside():
        for side, src, dst in features:
            got.setdefault(side, []).append(push(src, dst, device(core=other)))
        ps[z, core] = proto_s[...].T.astype(BF16)
        pt[z, core] = proto_t[...].T.astype(BF16)
        yield
        yield
        steps = [gather("z", lambda c, ref=ref: ref.at[c, core]) for ref in (ps, pt)]
        for step in steps:
            next(step)
        yield
        yield
        for step in steps:
            next(step)
        yield
        for copy in mine[0]:
            copy.wait_send()
        for a in range(2):
            for b in range(2):
                block = fx[0, a, :, pl.ds(768 * b, 768)].T
                w[a, b, :, :, :, 0:256] = block.reshape(4, 4, 48, 256)
        yield
        for step in steps:
            run(step)
        swaps = [push(ref.at[:, core], ref.at[:, core], device(core=other)) for ref in (ps, pt)]
        yield
        for copy in swaps:
            copy.wait_recv()
        for b in range(NB):
            pn[:, b * PB : (b + 1) * PB] = ps[b // 2, b % 2].T

    run(forward(0), forward(1), beside())

    sent = [push(tx.at[x], tx.at[x], device(x=lax.rem(x + d, 4))) for d in (1, 2, 3)]
    for copy in sent:
        copy.wait_recv()
    ty[y] = tx[0] + tx[1] + tx[2] + tx[3]
    sent = [push(ty.at[y], ty.at[y], device(y=lax.rem(y + d, 4))) for d in (1, 2, 3)]
    for copy in sent:
        copy.wait_recv()
    tot[...] = (1.0 / tau_student) / (ty[0] + ty[1] + ty[2] + ty[3])

    def back(a, h):
        i = a * 2 + h
        inv_s = jnp.concatenate([tot[0, pl.ds(2 * i, 1), :], tot[0, pl.ds(2 * i + 1, 1), :]], 1)
        inv_t = jnp.concatenate([tot[1, pl.ds(2 * i, 1), :], tot[1, pl.ds(2 * i + 1, 1), :]], 1)
        columns = pl.ds(pl.multiple_of(i * 2 * TB, 2 * TB), 2 * TB)
        dh = jnp.zeros((256, 2 * TB), F32)
        for b in range(NB):
            rows = pl.ds(b * PB, PB)
            d = (es[a, h, rows, :] * inv_s - et[a, h, rows, :] * inv_t).astype(BF16)
            dz[rows, columns] = d
            dh += dot(pn[:, rows], d)
        for d in range(2):
            dh0[0, a, 2 * h + d] = dh[:128, d * TB : (d + 1) * TB].astype(BF16)
            dh0[1, 2 * h + d, a] = dh[128:, d * TB : (d + 1) * TB].astype(BF16)

    sent = []
    for i, d in enumerate((2, 1, 3, 0)):
        to = lax.rem(x + d, 4)

        def half(h, _, to=to):
            back(to, h)
            return 0

        lax.fori_loop(0, 2, half, 0)
        if d > 0:
            sent.append(push(dh0.at[0, to], dhr0.at[0, i], device(x=to)))

    def dh_scatter(k):
        def middle(v):
            dh1[k] = v

        def last(v):
            dht[k] = v

        if k == 0:
            yield
            total = dh0[0, x].astype(F32)
            for i, copy in enumerate(sent):
                copy.wait_recv()
                total += dhr0[0, i].astype(F32)
            middle(total)
        else:
            yield from scatter("y", dh0.at[1], dhr0.at[1], middle)
        yield from scatter("yx"[k], dh1.at[k], dhr1.at[k], last)

    def proto_grad():
        def grad(block):
            rows = pl.ds(pl.multiple_of(block * PB, PB), PB)
            return dot(dz[rows, :], cs[...].reshape(NT, 256))

        def theirs(i, _):
            es[0, 0, pl.ds(pl.multiple_of(i * PB, PB), PB), :] = grad(i * 2 + other)
            return 0

        def ours(i, _):
            es[0, 1, pl.ds(pl.multiple_of(i * PB, PB), PB), :] = grad(i * 2 + core)
            return 0

        lax.fori_loop(0, 4, theirs, 0)
        swap = push(es.at[0, 0, pl.ds(0, 4 * PB), :], grecv, device(core=other))
        yield
        lax.fori_loop(0, 4, ours, 0)
        swap.wait_recv()
        gz[...] = (es[0, 1, : 4 * PB, :] + grecv[...]).astype(BF16).reshape(4, PB, 256)

        def last(v):
            g_proto[...] = v.T

        yield from scatter("z", gz, gzr, last)

    proto_steps = proto_grad()
    dh_steps = together(dh_scatter(0), dh_scatter(1))
    next(dh_steps)
    next(proto_steps)
    next(dh_steps)
    next(proto_steps)
    run(dh_steps)

    dhv = jnp.concatenate([dht[0], dht[1]], axis=0)
    u = unit[...]
    dyt = (dhv - u * jnp.sum(u * dhv, axis=0, keepdims=True)) / norm[0:1, :]
    dy[core] = dyt.astype(BF16)
    swap = push(dy.at[core], dy.at[core], device(core=other))
    swap.wait_recv()

    dyb = jnp.concatenate([dy[0], dy[1]], axis=1)
    for a in range(2):
        for b in range(2):
            c = b * 2 + a
            g = dot(w[a, b, :, :, :, 0:256].reshape(768, 256), dyb, ((1,), (1,))).astype(BF16)
            g = g.reshape(4, 4, 48, 256)
            for i in range(4):
                for j in range(4):
                    b0[0, i, j, c] = g[i, j, 0:16]
                    b0[1, j, c, i] = g[i, j, 16:32]
                    b0[2, c, i, j] = g[i, j, 32:48]

    def bot_scatter(k):
        def first(v):
            b1[k] = v

        def second(v):
            b2[k] = v

        def last(v):
            g_bot[16 * k : 16 * (k + 1), :] = v

        one, two, three = ("xyz", "yzx", "zxy")[k]
        yield from scatter(one, b0.at[k], br0.at[k], first)
        yield from scatter(two, b1.at[k], br1.at[k], second)
        yield from scatter(three, b2.at[k], br2.at[k], last)

    run(bot_scatter(0), bot_scatter(1), bot_scatter(2), proto_steps)
    for copy in copies:
        if not any(copy is one for one in mine[0]):
            copy.wait_send()


def gradients(feat_s, feat_t, bot_s, bot_t, proto_s, proto_t):
    whole = pl.BlockSpec(memory_space=pltpu.VMEM)
    vmem = pltpu.VMEM
    return pl.pallas_call(
        kernel,
        out_shape=(
            jax.ShapeDtypeStruct((48, 256), F32),
            jax.ShapeDtypeStruct((256, PB), F32),
        ),
        in_specs=[pl.BlockSpec(memory_space=pl.ANY)] * 2 + [whole] * 4,
        out_specs=(whole, whole),
        scratch_shapes=[
            vmem((2, 2, 4, 4, 48, 512), BF16),
            vmem((2, 2, 2 * TB, 1536), BF16),
            vmem((2, 2, TB, 256), F32),
            vmem((2, TB, 256), F32),
            vmem((256, TB), F32),
            vmem((8, TB), F32),
            vmem((4, 4, TB, 256), BF16),
            vmem((4, 4, TB, 256), BF16),
            vmem((4, 2, PB, 256), BF16),
            vmem((4, 2, PB, 256), BF16),
            vmem((256, NP), BF16),
            vmem((4, 2, NP, 2 * TB), F32),
            vmem((4, 2, NP, 2 * TB), F32),
            vmem((NP, NT), BF16),
            vmem((4, 2, 16, TB), F32),
            vmem((4, 2, 16, TB), F32),
            vmem((2, 16, TB), F32),
            vmem((2, 4, 4, 128, TB), BF16),
            vmem((2, 3, 4, 128, TB), BF16),
            vmem((2, 4, 128, TB), F32),
            vmem((2, 3, 128, TB), F32),
            vmem((2, 128, TB), F32),
            vmem((4 * PB, 256), F32),
            vmem((4, PB, 256), BF16),
            vmem((3, PB, 256), BF16),
            vmem((2, 256, TB), BF16),
            vmem((3, 4, 4, 4, 16, 256), BF16),
            vmem((3, 3, 4, 4, 16, 256), BF16),
            vmem((3, 4, 4, 16, 256), F32),
            vmem((3, 3, 4, 16, 256), F32),
            vmem((3, 4, 16, 256), F32),
            vmem((3, 3, 16, 256), F32),
            pltpu.SemaphoreType.DMA((SEMS,)),
            pltpu.SemaphoreType.DMA((SEMS,)),
            pltpu.SemaphoreType.DMA((4,)),
        ],
        compiler_params=pltpu.CompilerParams(
            collective_id=0, has_side_effects=True, vmem_limit_bytes=63 * 1024 * 1024
        ),
    )(feat_s, feat_t, bot_s, bot_t, proto_s, proto_t)


def per_device(feat_s, feat_t, bot_s, bot_m, bot_v, bot_t, proto_s, proto_m, proto_v, proto_t):
    g_bot, g_proto = gradients(feat_s, feat_t, bot_s, bot_t, proto_s, proto_t)
    return adamw(bot_s, bot_m, bot_v, g_bot, bot_t) + adamw(
        proto_s, proto_m, proto_v, g_proto, proto_t
    )


def solution(mesh):
    rows, columns = P(("dp", "fsdp"), None), P(None, ("fsdp", "dp"))
    return jax.shard_map(
        per_device,
        mesh=mesh,
        in_specs=(rows,) * 6 + (columns,) * 4,
        out_specs=(rows,) * 4 + (columns,) * 4,
        check_vma=False,
    )
```

time: 138 us -> 104 us (0.75)
  Pallas kernels: 134 us -> 100 us
    pallas_call x1, Pallas kernels: 134 us -> 100 us  [gradients(): pl.pallas_call(kernel, out_shape=(jax.ShapeDtypeStruct((48, 256), F32), j...]
where the time goes in v2:
time: 104 us
  Pallas kernels  100 us (96%)
  other arithmetic  2.86 us (3%)
    pallas_call x1, Pallas kernels, gradients(): pl.pallas_call(kernel, out_shape=(jax.ShapeDtypeStruct((48, 256), F32), j...  100 us
    add x2, other arithmetic, adamw(): teacher_new = 0.996 * teacher + 0.004 * param_new  2.86 us

profile of v2, /device:TPU:0, one launch (start us, length us, event | category | flops | bytes accessed | tf_op | source)
XLA Modules:
  0.0 103.7 jit_solution(1434126712307851037)
XLA Ops:
  0.6 0.0 copy-start
  0.6 0.0 copy-start.1
  0.7 0.0 copy-start.2
  0.7 100.0 %shard_map.161 = (f32[48,256]{1,0:T(8,128)}, f32[256,256]{1,0:T(8,128)}) custom-call(bf16[128,6144]{1,0:T(8,128)(2,1)} %feat_s.1, bf16[128,6144]{1,0:T(8,128)(2,1)} %feat_t.1, f32[48,256]{1,0:T(8,128)} %bot_s.1, f32[48,256]{1,0:T(8,128)} %bot_t.1, f32[256,256]{1,0:T(8,128)} %proto_s.1, f32[256,256]{1,0:T(8,128)} %proto_t.1), custom_call_target="tpu_custom_call" | custom-call | tf_op jit(solution)/shard_map/pallas_call | solution.py:429
  100.7 0.0 copy-start.3
  100.7 0.0 copy-start.4
  100.7 0.0 copy-start.5
  100.7 0.0 copy-start.6
  100.7 0.0 copy-start.7
  100.7 0.0 copy-done
  100.8 0.0 copy-done.1
  100.8 0.0 copy-done.2
  100.8 2.2 %multiply_add_fusion = (f32[256,256]{1,0:T(8,128)}, f32[256,256]{1,0:T(8,128)}, f32[256,256]{1,0:T(8,128)}, f32[256,256]{1,0:T(8,128)}) fusion(f32[256,256]{1,0:T(8,128)S(1)} %copy-done.1, f32[256,256]{1,0:T(8,128)S(1)} %copy-done, f32[256,256]{1,0:T(8,128)} %get-tuple-element.11, f32[256,256]{1,0:T(8,128)S(1)} %copy-done.2, f32[256,256]{1,0:T(8,128)} %param.18), kind=kLoop, calls=%fused_computation.2 | loop fusion | flops 1179648 | bytes 2359296 | tf_op jit(solution)/shard_map/add | solution.py:30
  102.9 0.0 copy-done.3
  102.9 0.0 copy-done.4
  102.9 0.0 copy-done.5
  102.9 0.0 copy-done.6
  103.0 0.0 copy-done.7
  103.0 0.7 multiply_add_fusion.2
Async XLA Ops:
  0.6 100.1 %copy-start = (f32[256,256]{1,0:T(8,128)S(1)}, f32[256,256]{1,0:T(8,128)}, u32[]{:S(2)}) copy-start(f32[256,256]{1,0:T(8,128)} %proto_s.1) | copy-start | bytes 786436
  0.6 100.1 %copy-start.1 = (f32[256,256]{1,0:T(8,128)S(1)}, f32[256,256]{1,0:T(8,128)}, u32[]{:S(2)}) copy-start(f32[256,256]{1,0:T(8,128)} %proto_t.1) | copy-start | bytes 786436
  0.7 100.1 %copy-start.2 = (f32[256,256]{1,0:T(8,128)S(1)}, f32[256,256]{1,0:T(8,128)}, u32[]{:S(2)}) copy-start(f32[256,256]{1,0:T(8,128)} %param.17) | copy-start | bytes 786436
  100.7 2.3 %copy-start.3 = (f32[48,256]{1,0:T(8,128)S(1)}, f32[48,256]{1,0:T(8,128)}, u32[]{:S(2)}) copy-start(f32[48,256]{1,0:T(8,128)} %bot_t.1) | copy-start | bytes 147460
  100.7 2.2 %copy-start.4 = (f32[48,256]{1,0:T(8,128)S(1)}, f32[48,256]{1,0:T(8,128)}, u32[]{:S(2)}) copy-start(f32[48,256]{1,0:T(8,128)} %bot_s.1) | copy-start | bytes 147460
  100.7 2.2 %copy-start.5 = (f32[48,256]{1,0:T(8,128)S(1)}, f32[48,256]{1,0:T(8,128)}, u32[]{:S(2)}) copy-start(f32[48,256]{1,0:T(8,128)} %param.13) | copy-start | bytes 147460
  100.7 2.2 %copy-start.6 = (f32[48,256]{1,0:T(8,128)S(1)}, f32[48,256]{1,0:T(8,128)}, u32[]{:S(2)}) copy-start(f32[48,256]{1,0:T(8,128)} %param.14) | copy-start | bytes 147460
  100.7 2.2 %copy-start.7 = (f32[48,256]{1,0:T(8,128)S(1)}, f32[48,256]{1,0:T(8,128)}, u32[]{:S(2)}) copy-start(f32[48,256]{1,0:T(8,128)} %get-tuple-element.10) | copy-start | bytes 147460

commit v3 on v2

--- a/solution.py
+++ b/solution.py
@@ -19,7 +19,7 @@
 NP = PB * NB
 TB = 128
 NT = 16 * TB
-SEMS = 160
+SEMS = 232
 
 
 def adamw(param, first, second, grad, teacher):
@@ -53,7 +53,8 @@
 
 def kernel(
     feat_s, feat_t, bot_s, bot_t, proto_s, proto_t,
-    g_bot, g_proto,
+    g_bot_out, g_proto_out,
+    bots, protos, g_bot, g_proto,
     w, fx, yf, yr, unit, norm, cs, ct, ps, pt, pn, es, et, dz,
     tx, ty, tot, dh0, dhr0, dh1, dhr1, dht, grecv, gz, gzr,
     dy, b0, br0, b1, br1, b2, br2,
@@ -123,6 +124,18 @@
             total += recv[i].astype(F32)
         put(total)
 
+    def load(src, dst, at):
+        copy = pltpu.make_async_copy(src, dst, local_sem.at[at])
+        copy.start()
+        return copy
+
+    loads = [
+        load(bot_s, bots.at[0], 4),
+        load(bot_t, bots.at[1], 5),
+        load(proto_s, protos.at[0], 6),
+        load(proto_t, protos.at[1], 7),
+    ]
+
     barrier = pltpu.get_barrier_semaphore()
     peers = [device(core=other)]
     for axis in ("x", "y", "z"):
@@ -136,13 +149,11 @@
         for half in range(2):
             columns = pl.ds(pl.multiple_of((half * 2 + core) * 1536, 1536), 1536)
             rows = pl.ds(pl.multiple_of(core * TB, TB), TB)
-            copy = pltpu.make_async_copy(
-                feat.at[:, columns], fx.at[side, half, rows, :], local_sem.at[side * 2 + half]
-            )
-            copy.start()
-            local.append(copy)
-    w[zl, zh, x, y, :, 0:256] = bot_s[...].astype(BF16)
-    w[zl, zh, x, y, :, 256:512] = bot_t[...].astype(BF16)
+            local.append(load(feat.at[:, columns], fx.at[side, half, rows, :], side * 2 + half))
+    loads[0].wait()
+    loads[1].wait()
+    w[zl, zh, x, y, :, 0:256] = bots[0].astype(BF16)
+    w[zl, zh, x, y, :, 256:512] = bots[1].astype(BF16)
     pl.semaphore_wait(barrier, len(peers))
 
     def part(k):
@@ -151,24 +162,38 @@
     mine = {0: [], 1: []}
 
     def bot_gather(k, side):
-        r, c = part(k), pl.ds(256 * side, 256)
-
-        def at_z(i):
-            return lax.rem(i, 2), lax.div(i, 2)
-
-        log = mine[side]
-        if k == 0:
-            yield from spread("x", lambda i: w.at[zl, zh, i, y, r, c], log)
-            yield from spread("y", lambda i: w.at[zl, zh, :, i, r, c], log)
-            yield from gather("z", lambda i: w.at[(*at_z(i), slice(None), slice(None), r, c)], log)
-        elif k == 1:
-            yield from spread("y", lambda i: w.at[zl, zh, x, i, r, c], log)
-            yield from spread("z", lambda i: w.at[(*at_z(i), x, slice(None), r, c)], log)
-            yield from gather("x", lambda i: w.at[:, :, i, :, r, c], log)
-        else:
-            yield from spread("z", lambda i: w.at[(*at_z(i), x, y, r, c)], log)
-            yield from spread("x", lambda i: w.at[:, :, i, y, r, c], log)
-            yield from gather("y", lambda i: w.at[:, :, :, i, r, c], log)
+        log, columns, every = mine[side], pl.ds(256 * side, 256), slice(None)
+        one, two, three = ("xyz", "yzx", "zxy")[k]
+
+        def block(**at):
+            at = {**place, **at}
+            zs = (every, every) if at["z"] is every else (lax.rem(at["z"], 2), lax.div(at["z"], 2))
+            return w.at[(*zs, at["x"], at["y"], part(k), columns)]
+
+        def send(ref, to, at):
+            return push(ref, ref, device(**{to: at}), log)
+
+        yield from spread(one, lambda i: block(**{one: i}), log)
+        at = place[two]
+        _, ahead, behind, _ = ring(three)
+        line = block(**{one: every})
+        sent = {d: send(line, two, lax.rem(at + d, 4)) for d in (2, 1, 3)}
+        up, down, lines = [send(line, three, ahead)], [send(line, three, behind)], [at]
+        yield
+        for d in (1, 3, 2):
+            sent[d].wait_recv()
+            lines.append(lax.rem(at + 4 - d, 4))
+            line = block(**{one: every, two: lines[-1]})
+            up.append(send(line, three, ahead))
+            down.append(send(line, three, behind))
+        yield
+        on = []
+        for copy, i in zip(up, lines):
+            copy.wait_recv()
+            on.append(send(block(**{one: every, two: i, three: behind}), three, ahead))
+        yield
+        for copy in down + on:
+            copy.wait_recv()
 
     features = []
     for side, feat in enumerate((feat_s, feat_t)):
@@ -237,24 +262,31 @@
 
     def forward(side):
         yield from projected(side)
-        if side == 0:
-            yield from spread("x", lambda i: cs.at[i, y])
-            axis, block = "y", lambda i, h: cs.at[pl.ds(2 * h, 2), i]
-        else:
-            yield from spread("y", lambda i: ct.at[x, i])
-            axis, block = "x", lambda i, h: ct.at[i, pl.ds(2 * h, 2)]
-        at, ahead, behind, far = ring(axis)
-        up = [push(block(at, h), block(at, h), device(**{axis: ahead})) for h in range(2)]
-        down = [push(block(at, h), block(at, h), device(**{axis: behind})) for h in range(2)]
+        one, two = ("xy", "yx")[side]
+        code = (cs, ct)[side]
+
+        def send(i, j, to, at):
+            ref = code.at[i, j] if side == 0 else code.at[j, i]
+            return push(ref, ref, device(**{to: at}))
+
+        first = place[one]
+        at, ahead, behind, far = ring(two)
+        sent = {d: send(first, at, one, lax.rem(first + d, 4)) for d in (2, 1, 3)}
+        up, down, lines = [send(first, at, two, ahead)], [send(first, at, two, behind)], [first]
+        yield
+        for d in (1, 3, 2):
+            sent[d].wait_recv()
+            lines.append(lax.rem(first + 4 - d, 4))
+            up.append(send(lines[-1], at, two, ahead))
+            down.append(send(lines[-1], at, two, behind))
         yield
         on = []
-        for h in range(2):
-            up[h].wait_recv()
-            on.append(push(block(behind, h), block(behind, h), device(**{axis: ahead})))
+        for copy, i in zip(up, lines):
+            copy.wait_recv()
+            on.append(send(i, behind, two, ahead))
         yield
         exponentials(side, at)
         exponentials(side, behind)
-        yield
         for copy in down:
             copy.wait_recv()
         exponentials(side, ahead)
@@ -266,8 +298,11 @@
     def beside():
         for side, src, dst in features:
             got.setdefault(side, []).append(push(src, dst, device(core=other)))
-        ps[z, core] = proto_s[...].T.astype(BF16)
-        pt[z, core] = proto_t[...].T.astype(BF16)
+        loads[2].wait()
+        loads[3].wait()
+        ps[z, core] = protos[0].T.astype(BF16)
+        pt[z, core] = protos[1].T.astype(BF16)
+        yield
         yield
         yield
         steps = [gather("z", lambda c, ref=ref: ref.at[c, core]) for ref in (ps, pt)]
@@ -275,8 +310,6 @@
             next(step)
         yield
         yield
-        for step in steps:
-            next(step)
         yield
         for copy in mine[0]:
             copy.wait_send()
@@ -284,6 +317,8 @@
             for b in range(2):
                 block = fx[0, a, :, pl.ds(768 * b, 768)].T
                 w[a, b, :, :, :, 0:256] = block.reshape(4, 4, 48, 256)
+        for step in steps:
+            next(step)
         yield
         for step in steps:
             run(step)
@@ -296,11 +331,11 @@
 
     run(forward(0), forward(1), beside())
 
-    sent = [push(tx.at[x], tx.at[x], device(x=lax.rem(x + d, 4))) for d in (1, 2, 3)]
+    sent = [push(tx.at[x], tx.at[x], device(x=lax.rem(x + d, 4))) for d in (2, 1, 3)]
     for copy in sent:
         copy.wait_recv()
     ty[y] = tx[0] + tx[1] + tx[2] + tx[3]
-    sent = [push(ty.at[y], ty.at[y], device(y=lax.rem(y + d, 4))) for d in (1, 2, 3)]
+    sent = [push(ty.at[y], ty.at[y], device(y=lax.rem(y + d, 4))) for d in (2, 1, 3)]
     for copy in sent:
         copy.wait_recv()
     tot[...] = (1.0 / tau_student) / (ty[0] + ty[1] + ty[2] + ty[3])
@@ -316,21 +351,28 @@
             d = (es[a, h, rows, :] * inv_s - et[a, h, rows, :] * inv_t).astype(BF16)
             dz[rows, columns] = d
             dh += dot(pn[:, rows], d)
+        dh = dh.astype(BF16)
         for d in range(2):
-            dh0[0, a, 2 * h + d] = dh[:128, d * TB : (d + 1) * TB].astype(BF16)
-            dh0[1, 2 * h + d, a] = dh[128:, d * TB : (d + 1) * TB].astype(BF16)
-
-    sent = []
-    for i, d in enumerate((2, 1, 3, 0)):
-        to = lax.rem(x + d, 4)
-
-        def half(h, _, to=to):
+            columns = slice(d * TB, (d + 1) * TB)
+            dh0[0, a, 2 * h + d] = dh[:128, columns]
+            dh0[1, 2 * h + d, a] = dh[128:, columns]
+
+    sent, sent_y = [], []
+    own, odd = lax.div(y, 2), lax.rem(y, 2)
+    for h in (1 - own, own):
+        for i, d in enumerate((2, 1, 3, 0)):
+            to = lax.rem(x + d, 4)
             back(to, h)
-            return 0
-
-        lax.fori_loop(0, 2, half, 0)
-        if d > 0:
-            sent.append(push(dh0.at[0, to], dhr0.at[0, i], device(x=to)))
+            if d > 0:
+                two = pl.ds(2 * h, 2)
+                sent.append(push(dh0.at[0, to, two], dhr0.at[0, i, two], device(x=to)))
+        if h is own:
+            to = 2 * own + 1 - odd
+            sent_y.append(push(dh0.at[1, to], dhr0.at[1, 0], device(y=to)))
+        else:
+            for e in range(2):
+                to = 2 * h + lax.rem(odd + e, 2)
+                sent_y.append(push(dh0.at[1, to], dhr0.at[1, 1 + e], device(y=to)))
 
     def dh_scatter(k):
         def middle(v):
@@ -339,15 +381,12 @@
         def last(v):
             dht[k] = v
 
-        if k == 0:
-            yield
-            total = dh0[0, x].astype(F32)
-            for i, copy in enumerate(sent):
-                copy.wait_recv()
-                total += dhr0[0, i].astype(F32)
-            middle(total)
-        else:
-            yield from scatter("y", dh0.at[1], dhr0.at[1], middle)
+        for copy in (sent, sent_y)[k]:
+            copy.wait_recv()
+        total = dh0[k, (x, y)[k]].astype(F32)
+        for i in range(3):
+            total += dhr0[k, i].astype(F32)
+        middle(total)
         yield from scatter("yx"[k], dh1.at[k], dhr1.at[k], last)
 
     def proto_grad():
@@ -372,19 +411,20 @@
 
         def last(v):
             g_proto[...] = v.T
+            stores.append(load(g_proto, g_proto_out, 8))
 
         yield from scatter("z", gz, gzr, last)
 
+    stores = []
     proto_steps = proto_grad()
     dh_steps = together(dh_scatter(0), dh_scatter(1))
-    next(dh_steps)
     next(proto_steps)
     next(dh_steps)
     next(proto_steps)
     run(dh_steps)
 
+    u = unit[...]
     dhv = jnp.concatenate([dht[0], dht[1]], axis=0)
-    u = unit[...]
     dyt = (dhv - u * jnp.sum(u * dhv, axis=0, keepdims=True)) / norm[0:1, :]
     dy[core] = dyt.astype(BF16)
     swap = push(dy.at[core], dy.at[core], device(core=other))
@@ -398,33 +438,37 @@
             g = g.reshape(4, 4, 48, 256)
             for i in range(4):
                 for j in range(4):
-                    b0[0, i, j, c] = g[i, j, 0:16]
-                    b0[1, j, c, i] = g[i, j, 16:32]
-                    b0[2, c, i, j] = g[i, j, 32:48]
-
-    def bot_scatter(k):
+                    for h in range(2):
+                        columns = slice(128 * h, 128 * (h + 1))
+                        b0[h, 0, i, j, c] = g[i, j, 0:16, columns]
+                        b0[h, 1, j, c, i] = g[i, j, 16:32, columns]
+                        b0[h, 2, c, i, j] = g[i, j, 32:48, columns]
+
+    def bot_scatter(k, h):
         def first(v):
-            b1[k] = v
+            b1[h, k] = v
 
         def second(v):
-            b2[k] = v
+            b2[h, k] = v
 
         def last(v):
-            g_bot[16 * k : 16 * (k + 1), :] = v
+            g_bot[16 * k : 16 * (k + 1), 128 * h : 128 * (h + 1)] = v
 
         one, two, three = ("xyz", "yzx", "zxy")[k]
-        yield from scatter(one, b0.at[k], br0.at[k], first)
-        yield from scatter(two, b1.at[k], br1.at[k], second)
-        yield from scatter(three, b2.at[k], br2.at[k], last)
-
-    run(bot_scatter(0), bot_scatter(1), bot_scatter(2), proto_steps)
+        yield from scatter(one, b0.at[h, k], br0.at[h, k], first)
+        yield from scatter(two, b1.at[h, k], br1.at[h, k], second)
+        yield from scatter(three, b2.at[h, k], br2.at[h, k], last)
+
+    run(*(bot_scatter(k, h) for h in range(2) for k in range(3)), proto_steps)
+    stores.append(load(g_bot, g_bot_out, 9))
     for copy in copies:
         if not any(copy is one for one in mine[0]):
             copy.wait_send()
+    for copy in stores:
+        copy.wait()
 
 
 def gradients(feat_s, feat_t, bot_s, bot_t, proto_s, proto_t):
-    whole = pl.BlockSpec(memory_space=pltpu.VMEM)
     vmem = pltpu.VMEM
     return pl.pallas_call(
         kernel,
@@ -432,9 +476,13 @@
             jax.ShapeDtypeStruct((48, 256), F32),
             jax.ShapeDtypeStruct((256, PB), F32),
         ),
-        in_specs=[pl.BlockSpec(memory_space=pl.ANY)] * 2 + [whole] * 4,
-        out_specs=(whole, whole),
+        in_specs=[pl.BlockSpec(memory_space=pl.ANY)] * 6,
+        out_specs=(pl.BlockSpec(memory_space=pl.ANY),) * 2,
         scratch_shapes=[
+            vmem((2, 48, 256), F32),
+            vmem((2, 256, PB), F32),
+            vmem((48, 256), F32),
+            vmem((256, PB), F32),
             vmem((2, 2, 4, 4, 48, 512), BF16),
             vmem((2, 2, 2 * TB, 1536), BF16),
             vmem((2, 2, TB, 256), F32),
@@ -461,15 +509,15 @@
             vmem((4, PB, 256), BF16),
             vmem((3, PB, 256), BF16),
             vmem((2, 256, TB), BF16),
-            vmem((3, 4, 4, 4, 16, 256), BF16),
-            vmem((3, 3, 4, 4, 16, 256), BF16),
-            vmem((3, 4, 4, 16, 256), F32),
-            vmem((3, 3, 4, 16, 256), F32),
-            vmem((3, 4, 16, 256), F32),
-            vmem((3, 3, 16, 256), F32),
+            vmem((2, 3, 4, 4, 4, 16, 128), BF16),
+            vmem((2, 3, 3, 4, 4, 16, 128), BF16),
+            vmem((2, 3, 4, 4, 16, 128), F32),
+            vmem((2, 3, 3, 4, 16, 128), F32),
+            vmem((2, 3, 4, 16, 128), F32),
+            vmem((2, 3, 3, 16, 128), F32),
             pltpu.SemaphoreType.DMA((SEMS,)),
             pltpu.SemaphoreType.DMA((SEMS,)),
-            pltpu.SemaphoreType.DMA((4,)),
+            pltpu.SemaphoreType.DMA((10,)),
         ],
         compiler_params=pltpu.CompilerParams(
             collective_id=0, has_side_effects=True, vmem_limit_bytes=63 * 1024 * 1024

time: 104 us -> 97.9 us (0.941)
  Pallas kernels: 100 us -> 93.9 us
    pallas_call x1, Pallas kernels: 100 us -> 93.9 us  [gradients(): pl.pallas_call(kernel, out_shape=(jax.ShapeDtypeStruct((48, 256), F32), j...]
where the time goes in v3:
time: 97.9 us; the launch traced here: 97.6 us
  Pallas kernels  93.9 us (96%)
  other arithmetic  2.86 us (3%)
    pallas_call x1, Pallas kernels, gradients(): pl.pallas_call(kernel, out_shape=(jax.ShapeDtypeStruct((48, 256), F32), j...  93.9 us
    add x2, other arithmetic, adamw(): teacher_new = 0.996 * teacher + 0.004 * param_new  2.86 us

profile of v3, /device:TPU:0, one launch (start us, length us, event | category | flops | bytes accessed | tf_op | source)
XLA Modules:
  0.0 97.6 jit_solution(2205422084024247642)
XLA Ops:
  0.6 0.0 copy-start
  0.6 0.0 copy-start.1
  0.7 0.0 copy-start.2
  0.7 93.9 %shard_map.161 = (f32[48,256]{1,0:T(8,128)}, f32[256,256]{1,0:T(8,128)}) custom-call(bf16[128,6144]{1,0:T(8,128)(2,1)} %feat_s.1, bf16[128,6144]{1,0:T(8,128)(2,1)} %feat_t.1, f32[48,256]{1,0:T(8,128)} %bot_s.1, f32[48,256]{1,0:T(8,128)} %bot_t.1, f32[256,256]{1,0:T(8,128)} %proto_s.1, f32[256,256]{1,0:T(8,128)} %proto_t.1), custom_call_target="tpu_custom_call" | custom-call | tf_op jit(solution)/shard_map/pallas_call | solution.py:473
  94.6 0.0 copy-start.3
  94.6 0.0 copy-start.4
  94.6 0.0 copy-start.5
  94.7 0.0 copy-start.6
  94.7 0.0 copy-start.7
  94.7 0.0 copy-done
  94.7 0.0 copy-done.1
  94.7 0.0 copy-done.2
  94.7 2.2 %multiply_add_fusion = (f32[256,256]{1,0:T(8,128)}, f32[256,256]{1,0:T(8,128)}, f32[256,256]{1,0:T(8,128)}, f32[256,256]{1,0:T(8,128)}) fusion(f32[256,256]{1,0:T(8,128)S(1)} %copy-done.1, f32[256,256]{1,0:T(8,128)S(1)} %copy-done, f32[256,256]{1,0:T(8,128)} %get-tuple-element.11, f32[256,256]{1,0:T(8,128)S(1)} %copy-done.2, f32[256,256]{1,0:T(8,128)} %param.18), kind=kLoop, calls=%fused_computation.2 | loop fusion | flops 1179648 | bytes 2359296 | tf_op jit(solution)/shard_map/add | solution.py:30
  96.9 0.0 copy-done.3
  96.9 0.0 copy-done.4
  96.9 0.0 copy-done.5
  96.9 0.0 copy-done.6
  96.9 0.0 copy-done.7
  96.9 0.7 multiply_add_fusion.2
Async XLA Ops:
  0.6 94.0 %copy-start = (f32[256,256]{1,0:T(8,128)S(1)}, f32[256,256]{1,0:T(8,128)}, u32[]{:S(2)}) copy-start(f32[256,256]{1,0:T(8,128)} %proto_s.1) | copy-start | bytes 786436
  0.6 94.0 %copy-start.1 = (f32[256,256]{1,0:T(8,128)S(1)}, f32[256,256]{1,0:T(8,128)}, u32[]{:S(2)}) copy-start(f32[256,256]{1,0:T(8,128)} %proto_t.1) | copy-start | bytes 786436
  0.7 94.0 %copy-start.2 = (f32[256,256]{1,0:T(8,128)S(1)}, f32[256,256]{1,0:T(8,128)}, u32[]{:S(2)}) copy-start(f32[256,256]{1,0:T(8,128)} %param.17) | copy-start | bytes 786436
  94.6 2.3 %copy-start.3 = (f32[48,256]{1,0:T(8,128)S(1)}, f32[48,256]{1,0:T(8,128)}, u32[]{:S(2)}) copy-start(f32[48,256]{1,0:T(8,128)} %bot_t.1) | copy-start | bytes 147460
  94.6 2.2 %copy-start.4 = (f32[48,256]{1,0:T(8,128)S(1)}, f32[48,256]{1,0:T(8,128)}, u32[]{:S(2)}) copy-start(f32[48,256]{1,0:T(8,128)} %bot_s.1) | copy-start | bytes 147460
  94.6 2.2 %copy-start.5 = (f32[48,256]{1,0:T(8,128)S(1)}, f32[48,256]{1,0:T(8,128)}, u32[]{:S(2)}) copy-start(f32[48,256]{1,0:T(8,128)} %param.13) | copy-start | bytes 147460
  94.7 2.2 %copy-start.6 = (f32[48,256]{1,0:T(8,128)S(1)}, f32[48,256]{1,0:T(8,128)}, u32[]{:S(2)}) copy-start(f32[48,256]{1,0:T(8,128)} %param.14) | copy-start | bytes 147460
  94.7 2.2 %copy-start.7 = (f32[48,256]{1,0:T(8,128)S(1)}, f32[48,256]{1,0:T(8,128)}, u32[]{:S(2)}) copy-start(f32[48,256]{1,0:T(8,128)} %get-tuple-element.10) | copy-start | bytes 147460

commit v4 on v3

--- a/solution.py
+++ b/solution.py
@@ -19,7 +19,7 @@
 NP = PB * NB
 TB = 128
 NT = 16 * TB
-SEMS = 232
+SEMS = 256
 
 
 def adamw(param, first, second, grad, teacher):
@@ -129,13 +129,6 @@
         copy.start()
         return copy
 
-    loads = [
-        load(bot_s, bots.at[0], 4),
-        load(bot_t, bots.at[1], 5),
-        load(proto_s, protos.at[0], 6),
-        load(proto_t, protos.at[1], 7),
-    ]
-
     barrier = pltpu.get_barrier_semaphore()
     peers = [device(core=other)]
     for axis in ("x", "y", "z"):
@@ -143,6 +136,13 @@
             peers.append(device(**{axis: lax.rem(place[axis] + step, 4)}))
     for peer in peers:
         pl.semaphore_signal(barrier, inc=1, device_id=peer, device_id_type=MESH)
+
+    loads = [
+        load(bot_s, bots.at[0], 4),
+        load(bot_t, bots.at[1], 5),
+        load(proto_s, protos.at[0], 6),
+        load(proto_t, protos.at[1], 7),
+    ]
 
     local = []
     for side, feat in enumerate((feat_s, feat_t)):
@@ -219,13 +219,9 @@
         swap = push(yf.at[side, other], yr.at[side], device(core=other))
         yield
         swap.wait_recv()
-        yt = (yf[side, core] + yr[side]).T
-        n = jnp.sqrt(jnp.sum(yt * yt, axis=0, keepdims=True) + 1e-06)
-        u = yt / n
-        if side == 0:
-            unit[...] = u
-            norm[0:1, :] = n
-        (cs, ct)[side][x, y] = u.T.astype(BF16)
+        v = yf[side, core] + yr[side]
+        n = jnp.sqrt(jnp.sum(v * v, axis=1, keepdims=True) + 1e-06)
+        (cs, ct)[side][x, y] = (v / n).astype(BF16)
 
     def exponentials(side, line):
         code, proto, out, scale = (
@@ -320,6 +316,10 @@
         for step in steps:
             next(step)
         yield
+        yt = (yf[0, core] + yr[0]).T
+        n = jnp.sqrt(jnp.sum(yt * yt, axis=0, keepdims=True) + 1e-06)
+        unit[...] = yt / n
+        norm[0:1, :] = n
         for step in steps:
             run(step)
         swaps = [push(ref.at[:, core], ref.at[:, core], device(core=other)) for ref in (ps, pt)]
@@ -357,37 +357,43 @@
             dh0[0, a, 2 * h + d] = dh[:128, columns]
             dh0[1, 2 * h + d, a] = dh[128:, columns]
 
-    sent, sent_y = [], []
     own, odd = lax.div(y, 2), lax.rem(y, 2)
-    for h in (1 - own, own):
-        for i, d in enumerate((2, 1, 3, 0)):
-            to = lax.rem(x + d, 4)
+    mate = 2 * own + 1 - odd
+    across = [2 * (1 - own) + lax.rem(odd + e, 2) for e in range(2)]
+    order = [(d, lax.rem(x + d, 4)) for d in (2, 1, 3, 0)]
+    sent, sent_y = [[], []], []
+    for n, h in enumerate((1 - own, own)):
+        two = pl.ds(2 * h, 2)
+        for i, (d, to) in enumerate(order):
             back(to, h)
             if d > 0:
-                two = pl.ds(2 * h, 2)
-                sent.append(push(dh0.at[0, to, two], dhr0.at[0, i, two], device(x=to)))
-        if h is own:
-            to = 2 * own + 1 - odd
-            sent_y.append(push(dh0.at[1, to], dhr0.at[1, 0], device(y=to)))
-        else:
-            for e in range(2):
-                to = 2 * h + lax.rem(odd + e, 2)
-                sent_y.append(push(dh0.at[1, to], dhr0.at[1, 1 + e], device(y=to)))
-
-    def dh_scatter(k):
-        def middle(v):
-            dh1[k] = v
-
-        def last(v):
-            dht[k] = v
-
-        for copy in (sent, sent_y)[k]:
-            copy.wait_recv()
-        total = dh0[k, (x, y)[k]].astype(F32)
-        for i in range(3):
-            total += dhr0[k, i].astype(F32)
-        middle(total)
-        yield from scatter("yx"[k], dh1.at[k], dhr1.at[k], last)
+                sent[n].append(push(dh0.at[0, to, two], dhr0.at[0, i, two], device(x=to)))
+            for slot, to_y in ((1, across[0]), (2, across[1])) if n == 0 else ((0, mate),):
+                sent_y.append(push(dh0.at[1, to_y, to], dhr0.at[1, slot, to], device(y=to_y)))
+
+    passed = [[], []]
+
+    def dh_rows(n):
+        for copy in sent[n]:
+            copy.wait_recv()
+        for slot, to in ((1, across[0]), (2, across[1])) if n == 0 else ((0, mate), (None, y)):
+            total = dh0[0, x, to].astype(F32)
+            for i in range(3):
+                total += dhr0[0, i, to].astype(F32)
+            dh1[0, to] = total
+            if slot is not None:
+                passed[0].append(push(dh1.at[0, to], dhr1.at[0, slot], device(y=to)))
+
+    def dh_columns(i):
+        d, to = order[i]
+        for at in (2 * i, 2 * i + 1, 8 + i):
+            sent_y[at].wait_recv()
+        total = dh0[1, y, to].astype(F32)
+        for slot in range(3):
+            total += dhr0[1, slot, to].astype(F32)
+        dh1[1, to] = total
+        if d > 0:
+            passed[1].append(push(dh1.at[1, to], dhr1.at[1, i], device(x=to)))
 
     def proto_grad():
         def grad(block):
@@ -417,11 +423,18 @@
 
     stores = []
     proto_steps = proto_grad()
-    dh_steps = together(dh_scatter(0), dh_scatter(1))
     next(proto_steps)
-    next(dh_steps)
+    dh_rows(0)
+    dh_columns(0)
+    dh_columns(1)
+    dh_rows(1)
+    dh_columns(2)
+    dh_columns(3)
     next(proto_steps)
-    run(dh_steps)
+    for k in range(2):
+        for copy in passed[k]:
+            copy.wait_recv()
+        dht[k] = dh1[k, (y, x)[k]] + dhr1[k, 0] + dhr1[k, 1] + dhr1[k, 2]
 
     u = unit[...]
     dhv = jnp.concatenate([dht[0], dht[1]], axis=0)

time: 97.9 us -> 97 us (level)
  no operation moved by 1% of the time
where the time goes in v4:
time: 97 us; the launch traced here: 96.9 us
  Pallas kernels  93.2 us (96%)
  other arithmetic  2.86 us (3%)
    pallas_call x1, Pallas kernels, gradients(): pl.pallas_call(kernel, out_shape=(jax.ShapeDtypeStruct((48, 256), F32), j...  93.2 us
    add x2, other arithmetic, adamw(): teacher_new = 0.996 * teacher + 0.004 * param_new  2.86 us

profile of v4, /device:TPU:0, one launch (start us, length us, event | category | flops | bytes accessed | tf_op | source)
XLA Modules:
  0.0 96.9 jit_solution(1674454983016104302)
XLA Ops:
  0.6 0.0 copy-start
  0.6 0.0 copy-start.1
  0.7 0.0 copy-start.2
  0.7 93.2 %shard_map.161 = (f32[48,256]{1,0:T(8,128)}, f32[256,256]{1,0:T(8,128)}) custom-call(bf16[128,6144]{1,0:T(8,128)(2,1)} %feat_s.1, bf16[128,6144]{1,0:T(8,128)(2,1)} %feat_t.1, f32[48,256]{1,0:T(8,128)} %bot_s.1, f32[48,256]{1,0:T(8,128)} %bot_t.1, f32[256,256]{1,0:T(8,128)} %proto_s.1, f32[256,256]{1,0:T(8,128)} %proto_t.1), custom_call_target="tpu_custom_call" | custom-call | tf_op jit(solution)/shard_map/pallas_call | solution.py:486
  93.9 0.0 copy-start.3
  93.9 0.0 copy-start.4
  93.9 0.0 copy-start.5
  93.9 0.0 copy-start.6
  93.9 0.0 copy-start.7
  93.9 0.0 copy-done
  93.9 0.0 copy-done.1
  94.0 0.0 copy-done.2
  94.0 2.2 %multiply_add_fusion = (f32[256,256]{1,0:T(8,128)}, f32[256,256]{1,0:T(8,128)}, f32[256,256]{1,0:T(8,128)}, f32[256,256]{1,0:T(8,128)}) fusion(f32[256,256]{1,0:T(8,128)S(1)} %copy-done.1, f32[256,256]{1,0:T(8,128)S(1)} %copy-done, f32[256,256]{1,0:T(8,128)} %get-tuple-element.11, f32[256,256]{1,0:T(8,128)S(1)} %copy-done.2, f32[256,256]{1,0:T(8,128)} %param.18), kind=kLoop, calls=%fused_computation.2 | loop fusion | flops 1179648 | bytes 2359296 | tf_op jit(solution)/shard_map/add | solution.py:30
  96.1 0.0 copy-done.3
  96.1 0.0 copy-done.4
  96.1 0.0 copy-done.5
  96.1 0.0 copy-done.6
  96.1 0.0 copy-done.7
  96.2 0.7 multiply_add_fusion.2
Async XLA Ops:
  0.6 93.3 %copy-start = (f32[256,256]{1,0:T(8,128)S(1)}, f32[256,256]{1,0:T(8,128)}, u32[]{:S(2)}) copy-start(f32[256,256]{1,0:T(8,128)} %proto_s.1) | copy-start | bytes 786436
  0.6 93.3 %copy-start.1 = (f32[256,256]{1,0:T(8,128)S(1)}, f32[256,256]{1,0:T(8,128)}, u32[]{:S(2)}) copy-start(f32[256,256]{1,0:T(8,128)} %proto_t.1) | copy-start | bytes 786436
  0.7 93.3 %copy-start.2 = (f32[256,256]{1,0:T(8,128)S(1)}, f32[256,256]{1,0:T(8,128)}, u32[]{:S(2)}) copy-start(f32[256,256]{1,0:T(8,128)} %param.17) | copy-start | bytes 786436
  93.9 2.3 %copy-start.3 = (f32[48,256]{1,0:T(8,128)S(1)}, f32[48,256]{1,0:T(8,128)}, u32[]{:S(2)}) copy-start(f32[48,256]{1,0:T(8,128)} %bot_t.1) | copy-start | bytes 147460
  93.9 2.2 %copy-start.4 = (f32[48,256]{1,0:T(8,128)S(1)}, f32[48,256]{1,0:T(8,128)}, u32[]{:S(2)}) copy-start(f32[48,256]{1,0:T(8,128)} %bot_s.1) | copy-start | bytes 147460
  93.9 2.2 %copy-start.5 = (f32[48,256]{1,0:T(8,128)S(1)}, f32[48,256]{1,0:T(8,128)}, u32[]{:S(2)}) copy-start(f32[48,256]{1,0:T(8,128)} %param.13) | copy-start | bytes 147460
  93.9 2.2 %copy-start.6 = (f32[48,256]{1,0:T(8,128)S(1)}, f32[48,256]{1,0:T(8,128)}, u32[]{:S(2)}) copy-start(f32[48,256]{1,0:T(8,128)} %param.14) | copy-start | bytes 147460
  93.9 2.2 %copy-start.7 = (f32[48,256]{1,0:T(8,128)S(1)}, f32[48,256]{1,0:T(8,128)}, u32[]{:S(2)}) copy-start(f32[48,256]{1,0:T(8,128)} %get-tuple-element.10) | copy-start | bytes 147460

commit v5 on v4

--- a/solution.py
+++ b/solution.py
@@ -451,28 +451,41 @@
             g = g.reshape(4, 4, 48, 256)
             for i in range(4):
                 for j in range(4):
-                    for h in range(2):
-                        columns = slice(128 * h, 128 * (h + 1))
-                        b0[h, 0, i, j, c] = g[i, j, 0:16, columns]
-                        b0[h, 1, j, c, i] = g[i, j, 16:32, columns]
-                        b0[h, 2, c, i, j] = g[i, j, 32:48, columns]
-
-    def bot_scatter(k, h):
-        def first(v):
-            b1[h, k] = v
-
-        def second(v):
-            b2[h, k] = v
+                    b0[0, i, j, c] = g[i, j, 0:16]
+                    b0[1, j, c, i] = g[i, j, 16:32]
+                    b0[2, c, i, j] = g[i, j, 32:48]
+
+    def bot_scatter(k):
+        one, two, three = ("xyz", "yzx", "zxy")[k]
+        at, next_at = place[one], place[two]
+        lines = [(d, lax.rem(next_at + d, 4)) for d in (2, 1, 3, 0)]
+        first, second = [], []
+        for _, j in lines:
+            for i, d in enumerate((2, 1, 3)):
+                to = lax.rem(at + d, 4)
+                first.append(push(b0.at[k, to, j], br0.at[k, i, j], device(**{one: to})))
+        yield
+        for n, (d, j) in enumerate(lines):
+            total = b0[k, at, j].astype(F32)
+            for i in range(3):
+                first[3 * n + i].wait_recv()
+                total += br0[k, i, j].astype(F32)
+            b1[k, j] = total
+            if d > 0:
+                second.append(push(b1.at[k, j], br1.at[k, n], device(**{two: j})))
+            yield
+        total = b1[k, next_at]
+        for i, copy in enumerate(second):
+            copy.wait_recv()
+            total += br1[k, i]
+        b2[k] = total
 
         def last(v):
-            g_bot[16 * k : 16 * (k + 1), 128 * h : 128 * (h + 1)] = v
-
-        one, two, three = ("xyz", "yzx", "zxy")[k]
-        yield from scatter(one, b0.at[h, k], br0.at[h, k], first)
-        yield from scatter(two, b1.at[h, k], br1.at[h, k], second)
-        yield from scatter(three, b2.at[h, k], br2.at[h, k], last)
-
-    run(*(bot_scatter(k, h) for h in range(2) for k in range(3)), proto_steps)
+            g_bot[16 * k : 16 * (k + 1), :] = v
+
+        yield from scatter(three, b2.at[k], br2.at[k], last)
+
+    run(*(bot_scatter(k) for k in range(3)), proto_steps)
     stores.append(load(g_bot, g_bot_out, 9))
     for copy in copies:
         if not any(copy is one for one in mine[0]):
@@ -522,12 +535,12 @@
             vmem((4, PB, 256), BF16),
             vmem((3, PB, 256), BF16),
             vmem((2, 256, TB), BF16),
-            vmem((2, 3, 4, 4, 4, 16, 128), BF16),
-            vmem((2, 3, 3, 4, 4, 16, 128), BF16),
-            vmem((2, 3, 4, 4, 16, 128), F32),
-            vmem((2, 3, 3, 4, 16, 128), F32),
-            vmem((2, 3, 4, 16, 128), F32),
-            vmem((2, 3, 3, 16, 128), F32),
+            vmem((3, 4, 4, 4, 16, 256), BF16),
+            vmem((3, 3, 4, 4, 16, 256), BF16),
+            vmem((3, 4, 4, 16, 256), F32),
+            vmem((3, 3, 4, 16, 256), F32),
+            vmem((3, 4, 16, 256), F32),
+            vmem((3, 3, 16, 256), F32),
             pltpu.SemaphoreType.DMA((SEMS,)),
             pltpu.SemaphoreType.DMA((SEMS,)),
             pltpu.SemaphoreType.DMA((10,)),

time: 97 us -> 95.5 us (0.985)
  Pallas kernels: 93.2 us -> 91.4 us
    pallas_call x1, Pallas kernels: 93.2 us -> 91.4 us  [gradients(): pl.pallas_call(kernel, out_shape=(jax.ShapeDtypeStruct((48, 256), F32), j...]
where the time goes in v5:
time: 95.5 us; the launch traced here: 95 us
  Pallas kernels  91.4 us (96%)
  other arithmetic  2.86 us (3%)
    pallas_call x1, Pallas kernels, gradients(): pl.pallas_call(kernel, out_shape=(jax.ShapeDtypeStruct((48, 256), F32), j...  91.4 us
    add x2, other arithmetic, adamw(): teacher_new = 0.996 * teacher + 0.004 * param_new  2.86 us

profile of v5, /device:TPU:0, one launch (start us, length us, event | category | flops | bytes accessed | tf_op | source)
XLA Modules:
  0.0 95.0 jit_solution(12366196687924001191)
XLA Ops:
  0.6 0.0 copy-start
  0.6 0.0 copy-start.1
  0.7 0.0 copy-start.2
  0.7 91.4 %shard_map.161 = (f32[48,256]{1,0:T(8,128)}, f32[256,256]{1,0:T(8,128)}) custom-call(bf16[128,6144]{1,0:T(8,128)(2,1)} %feat_s.1, bf16[128,6144]{1,0:T(8,128)(2,1)} %feat_t.1, f32[48,256]{1,0:T(8,128)} %bot_s.1, f32[48,256]{1,0:T(8,128)} %bot_t.1, f32[256,256]{1,0:T(8,128)} %proto_s.1, f32[256,256]{1,0:T(8,128)} %proto_t.1), custom_call_target="tpu_custom_call" | custom-call | tf_op jit(solution)/shard_map/pallas_call | solution.py:499
  92.0 0.0 copy-start.3
  92.0 0.0 copy-start.4
  92.1 0.0 copy-start.5
  92.1 0.0 copy-start.6
  92.1 0.0 copy-start.7
  92.1 0.0 copy-done
  92.1 0.0 copy-done.1
  92.1 0.0 copy-done.2
  92.1 2.2 %multiply_add_fusion = (f32[256,256]{1,0:T(8,128)}, f32[256,256]{1,0:T(8,128)}, f32[256,256]{1,0:T(8,128)}, f32[256,256]{1,0:T(8,128)}) fusion(f32[256,256]{1,0:T(8,128)S(1)} %copy-done.1, f32[256,256]{1,0:T(8,128)S(1)} %copy-done, f32[256,256]{1,0:T(8,128)} %get-tuple-element.11, f32[256,256]{1,0:T(8,128)S(1)} %copy-done.2, f32[256,256]{1,0:T(8,128)} %param.18), kind=kLoop, calls=%fused_computation.2 | loop fusion | flops 1179648 | bytes 2359296 | tf_op jit(solution)/shard_map/add | solution.py:30
  94.3 0.0 copy-done.3
  94.3 0.0 copy-done.4
  94.3 0.0 copy-done.5
  94.3 0.0 copy-done.6
  94.3 0.0 copy-done.7
  94.3 0.7 multiply_add_fusion.2
Async XLA Ops:
  0.6 91.5 %copy-start = (f32[256,256]{1,0:T(8,128)S(1)}, f32[256,256]{1,0:T(8,128)}, u32[]{:S(2)}) copy-start(f32[256,256]{1,0:T(8,128)} %proto_s.1) | copy-start | bytes 786436
  0.6 91.5 %copy-start.1 = (f32[256,256]{1,0:T(8,128)S(1)}, f32[256,256]{1,0:T(8,128)}, u32[]{:S(2)}) copy-start(f32[256,256]{1,0:T(8,128)} %proto_t.1) | copy-start | bytes 786436
  0.7 91.5 %copy-start.2 = (f32[256,256]{1,0:T(8,128)S(1)}, f32[256,256]{1,0:T(8,128)}, u32[]{:S(2)}) copy-start(f32[256,256]{1,0:T(8,128)} %param.17) | copy-start | bytes 786436
  92.0 2.3 %copy-start.3 = (f32[48,256]{1,0:T(8,128)S(1)}, f32[48,256]{1,0:T(8,128)}, u32[]{:S(2)}) copy-start(f32[48,256]{1,0:T(8,128)} %bot_t.1) | copy-start | bytes 147460
  92.0 2.2 %copy-start.4 = (f32[48,256]{1,0:T(8,128)S(1)}, f32[48,256]{1,0:T(8,128)}, u32[]{:S(2)}) copy-start(f32[48,256]{1,0:T(8,128)} %bot_s.1) | copy-start | bytes 147460
  92.1 2.2 %copy-start.5 = (f32[48,256]{1,0:T(8,128)S(1)}, f32[48,256]{1,0:T(8,128)}, u32[]{:S(2)}) copy-start(f32[48,256]{1,0:T(8,128)} %param.13) | copy-start | bytes 147460
  92.1 2.2 %copy-start.6 = (f32[48,256]{1,0:T(8,128)S(1)}, f32[48,256]{1,0:T(8,128)}, u32[]{:S(2)}) copy-start(f32[48,256]{1,0:T(8,128)} %param.14) | copy-start | bytes 147460
  92.1 2.2 %copy-start.7 = (f32[48,256]{1,0:T(8,128)S(1)}, f32[48,256]{1,0:T(8,128)}, u32[]{:S(2)}) copy-start(f32[48,256]{1,0:T(8,128)} %get-tuple-element.10) | copy-start | bytes 147460
